TPU v7x, 32 devices: a whole 2x2x4 slice. The times are simulated.
32 devices in a mesh: rep: 8 (over z, x), tp: 4 (over y, core).
Axes of the slice: x: 2, y: 2, z: 4, core: 2. Of those that a mesh axis runs over, the one named last changes fastest.
Arguments:
- x_in: bfloat16 [256, 16384], P('rep', 'tp'), may hold values from -6 to 6
- z_gate: bfloat16 [256, 16384], P('rep', 'tp'), may hold values from -6 to 6
- conv_state: bfloat16 [256, 3, 16384], P('rep', None, 'tp'), may hold values from -6 to 6
- conv_pool: bfloat16 [128, 3, 16384], P('rep', None, 'tp'), may hold values from -6 to 6
- ssm_state: float32 [256, 16, 16384], P('rep', None, 'tp'), may hold values from -6 to 6
- ssm_pool: float32 [128, 16, 16384], P('rep', None, 'tp'), may hold values from -6 to 6
- conv_weight: bfloat16 [4, 16384], P(None, 'tp'), may hold values from -3 to 3
- conv_bias: float32 [16384], P('tp'), may hold values from -0.5 to 0.5
- x_proj: bfloat16 [16384, 544], P('tp'), may hold values from -0.046875 to 0.046875
- dt_gain: float32 [512], replicated, may hold values from 0.5 to 1.5
- b_gain: float32 [16], replicated, may hold values from 0.5 to 1.5
- c_gain: float32 [16], replicated, may hold values from 0.5 to 1.5
- dt_proj: bfloat16 [512, 16384], P(None, 'tp'), may hold values from -0.25 to 0.25
- dt_bias: float32 [16384], P('tp'), may hold values from -3 to 0
- decay_rate: float32 [16, 16384], P(None, 'tp'), may hold values from 0.5 to 16
- skip: float32 [16384], P('tp'), may hold values from 0.5 to 1.5
- query: bfloat16 [256, 8192], P('rep', 'tp'), may hold values from -16 to 16
- new_kv: bfloat16 [256, 2048], P('rep', 'tp'), may hold values from -6 to 6
- kv_cache: bfloat16 [256, 512, 2048], P('rep', None, 'tp'), may hold values from -16 to 16
- kv_pool: bfloat16 [2048, 16, 2048], P('rep', None, 'tp'), may hold values from -16 to 16
- ctx_len: int32 [256], P('rep'), may hold values from 2 to 512
- row_owner: int32 [256], P('rep'), may hold values from -1 to 7, as said below
- row_pos: int32 [256], P('rep'), may hold values from 0 to 1, as said below
- swap_slot: int32 [8, 8, 2], P('rep'), may hold values from 0 to 15, as said below
- swap_lens: int32 [8, 8, 2], P('rep'), may hold values from 2 to 512
- swap_pages: int32 [8, 8, 2, 32], P('rep'), may hold values from 0 to 255
Outputs:
- mamba_out: bfloat16 [256, 16384], P('rep', 'tp')
- attn_out: bfloat16 [256, 8192], P('rep', 'tp')
- new_ssm: float32 [256, 16, 16384], P('rep', None, 'tp')
- new_conv: bfloat16 [256, 3, 16384], P('rep', None, 'tp')
Inputs may be any that keep to these rules, and one draw needn't show every extreme that they name: -1 marks a resident request; otherwise the group along rep whose pool holds it. Of one group's rows at most 2 name the same owner, and the pairs (row_owner, row_pos) of one group's resumed rows are distinct; in every draw some group resumes 2 requests from every owner. A resumed request of group g with owner o is entry [o, g, row_pos] of the owner's lists; entries that no request names are unused. `swap_slot`: slots of one owner are distinct. `swap_pages`: only the first ceil(length / 16) pages of a request are read; pages may be shared.
All inputs are finite; a program needn't handle non-finite values.
Results may differ from a plain program's by a relative error of at most 0.013.
Values may be sent and summed in bfloat16 or wider, within the bound.
A program may use at most 128 MiB of HBM per device.

v0:
```python
import math

import jax
import jax.numpy as jnp
from jax import lax
from jax.sharding import PartitionSpec as P

HD = 128


def attend_block(query_heads, context, ctx_lengths):
    item_count = query_heads.shape[0]
    kv_heads = query_heads.shape[1]
    head_width = query_heads.shape[3]
    kv_pairs = context.reshape(item_count, context.shape[1], kv_heads, 2, head_width)
    key_rows = kv_pairs[:, :, :, 0, :]
    value_rows = kv_pairs[:, :, :, 1, :]
    score_block = jnp.einsum(
        "nkgd,ntkd->nkgt", query_heads, key_rows, preferred_element_type=jnp.float32
    ) * (1.0 / math.sqrt(head_width))
    live_mask = (jnp.arange(context.shape[1])[None, :] < ctx_lengths[:, None])[:, None, None, :]
    masked = jnp.where(live_mask, score_block, -1e30)
    score_top = jnp.max(masked, axis=-1)
    prob_weights = jnp.where(live_mask, jnp.exp(masked - score_top[..., None]), 0.0).astype(
        jnp.bfloat16
    )
    prob_total = jnp.sum(prob_weights.astype(jnp.float32), axis=-1)
    attn_mix = jnp.einsum(
        "nkgt,ntkd->nkgd", prob_weights, value_rows, preferred_element_type=jnp.float32
    )
    return (attn_mix, score_top, prob_total)


def finish(query_heads, new_pairs, attn_mix, score_top, prob_total):
    item_count, kv_heads, q_groups, head_width = query_heads.shape
    kv_pairs = new_pairs.reshape(item_count, kv_heads, 2, head_width)
    new_score = jnp.einsum(
        "nkgd,nkd->nkg", query_heads, kv_pairs[:, :, 0, :], preferred_element_type=jnp.float32
    ) * (1.0 / math.sqrt(head_width))
    score_peak = jnp.maximum(score_top, new_score)
    old_scale = jnp.exp(score_top - score_peak)
    new_scale = jnp.exp(new_score - score_peak)
    numerator = attn_mix * old_scale[..., None] + new_scale[..., None] * kv_pairs[
        :, :, None, 1, :
    ].astype(jnp.float32)
    result = numerator / (prob_total * old_scale + new_scale)[..., None]
    return result.reshape(item_count, -1).astype(jnp.bfloat16)


def rms_scaled(values, gain):
    return (
        values * lax.rsqrt(jnp.mean(values * values, axis=-1, keepdims=True) + 1e-06) * gain
    ).astype(jnp.bfloat16)


def shards(
    x_in,
    z_gate,
    conv_state,
    conv_pool,
    ssm_state,
    ssm_pool,
    conv_weight,
    conv_bias,
    x_proj,
    dt_gain,
    b_gain,
    c_gain,
    dt_proj,
    dt_bias,
    decay_rate,
    skip,
    query,
    new_kv,
    kv_cache,
    kv_pool,
    ctx_len,
    row_owner,
    row_pos,
    swap_slot,
    swap_lens,
    swap_pages,
):
    peer_count = lax.axis_size("rep")
    row_count = x_in.shape[0]
    slot_cap = swap_slot.shape[2]
    entry_count = peer_count * slot_cap
    head_width = HD
    kv_width = kv_cache.shape[2]
    kv_heads = kv_width // (2 * head_width)
    q_groups = query.shape[1] // (head_width * kv_heads)
    query_heads = query.reshape(row_count, kv_heads, q_groups, head_width)
    slot_list = swap_slot[0].reshape(-1)
    page_list = swap_pages[0].reshape(-1)
    ssm_send = jnp.take(ssm_pool, slot_list, axis=0).reshape(
        (peer_count, slot_cap) + ssm_pool.shape[1:]
    )
    conv_send = jnp.take(conv_pool, slot_list, axis=0).reshape(
        (peer_count, slot_cap) + conv_pool.shape[1:]
    )
    resumed = row_owner >= 0
    where_from = jnp.where(resumed, row_owner * slot_cap + row_pos, 0)

    def pick_rows(local_rows, received):
        flat = received.reshape((entry_count,) + received.shape[2:])
        picked = jnp.take(flat, where_from, axis=0)
        flag = resumed.reshape((row_count,) + (1,) * (local_rows.ndim - 1))
        return jnp.where(flag, picked, local_rows)

    page_send = jnp.take(kv_pool, page_list, axis=0).reshape(peer_count, slot_cap, -1, kv_width)
    ssm_in, lens_in = (
        lax.all_to_all(ssm_send, "rep", split_axis=0, concat_axis=0, tiled=True),
        lax.all_to_all(
            swap_lens[0].astype(jnp.float32), "rep", split_axis=0, concat_axis=0, tiled=True
        ),
    )
    conv_in, pages_in = (
        lax.all_to_all(conv_send, "rep", split_axis=0, concat_axis=0, tiled=True),
        lax.all_to_all(page_send, "rep", split_axis=0, concat_axis=0, tiled=True),
    )
    context = pick_rows(kv_cache, pages_in)
    ctx_lengths = jnp.where(
        resumed, jnp.take(lens_in.reshape(-1), where_from).astype(jnp.int32), ctx_len
    )
    attn_mix, score_top, prob_total = attend_block(query_heads, context, ctx_lengths)
    prev_conv = pick_rows(conv_state, conv_in)
    prev_ssm = pick_rows(ssm_state, ssm_in)
    conv_window = jnp.concatenate([prev_conv, x_in[:, None, :]], axis=1)
    conv_sum = (
        jnp.sum(conv_window.astype(jnp.float32) * conv_weight.astype(jnp.float32)[None], axis=1)
        + conv_bias
    )
    mixed_in = jax.nn.silu(conv_sum).astype(jnp.bfloat16)
    proj_part = jnp.dot(mixed_in, x_proj, preferred_element_type=jnp.float32)
    proj = lax.psum(proj_part, "tp")
    dt_rank = dt_proj.shape[0]
    state_size = decay_rate.shape[0]
    dt_normed = rms_scaled(proj[:, :dt_rank], dt_gain)
    dt_step = jax.nn.softplus(
        jnp.dot(dt_normed, dt_proj, preferred_element_type=jnp.float32) + dt_bias
    )
    inject = rms_scaled(proj[:, dt_rank : dt_rank + state_size], b_gain).astype(jnp.float32)
    read_out = rms_scaled(proj[:, dt_rank + state_size :], c_gain).astype(jnp.float32)
    signal = mixed_in.astype(jnp.float32)
    new_ssm = (
        jnp.exp(-dt_step[:, None, :] * decay_rate[None]) * prev_ssm
        + (dt_step * signal)[:, None, :] * inject[:, :, None]
    )
    mamba_out = (
        (jnp.sum(read_out[:, :, None] * new_ssm, axis=1) + skip * signal)
        * jax.nn.silu(z_gate.astype(jnp.float32))
    ).astype(jnp.bfloat16)
    attn_out = finish(query_heads, new_kv, attn_mix, score_top, prob_total)
    return (mamba_out, attn_out, new_ssm, conv_window[:, 1:])


def solution(mesh):
    in_specs = (
        P("rep", "tp"),
        P("rep", "tp"),
        P("rep", None, "tp"),
        P("rep", None, "tp"),
        P("rep", None, "tp"),
        P("rep", None, "tp"),
        P(None, "tp"),
        P("tp"),
        P("tp", None),
        P(),
        P(),
        P(),
        P(None, "tp"),
        P("tp"),
        P(None, "tp"),
        P("tp"),
        P("rep", "tp"),
        P("rep", "tp"),
        P("rep", None, "tp"),
        P("rep", None, "tp"),
        P("rep"),
        P("rep"),
        P("rep"),
        P("rep", None, None),
        P("rep", None, None),
        P("rep", None, None, None),
    )
    out_specs = (P("rep", "tp"), P("rep", "tp"), P("rep", None, "tp"), P("rep", None, "tp"))
    return jax.shard_map(shards, mesh=mesh, in_specs=in_specs, out_specs=out_specs, check_vma=False)
```

profile of v0, /device:TPU:0, one launch (start us, length us, event | category | flops | bytes accessed | tf_op | source)
XLA Modules:
  0.0 395.5 jit_solution(15371303527826529770)
XLA Ops:
  7.2 0.0 copy-start
  7.2 0.7 convert_bitcast_fusion
  7.9 0.7 copy.103
  8.6 7.3 %all-to-all-start.2 = ((f32[8,1,2]{2,1,0:T(1,128)}), f32[8,1,2]{2,1,0:T(1,128)S(1)}, u32[]{:S(2)}, u32[]{:S(2)}) async-start(f32[8,1,2]{2,1,0:T(1,128)} %copy.103), calls=%async_computation.2 | async-start | bytes 8192 | tf_op jit(solution)/shard_map/all_to_all | solution.py:113
  15.8 0.8 copy.97
  16.6 0.7 compare_and_fusion.1
  17.3 0.1 reshape_squeeze.11
  17.4 1.7 gather_fusion
  19.1 0.3 gather.35
  19.3 0.1 copy.96
  19.4 1.2 broadcast_select_fusion.2
  20.6 5.0 %gather_fusion.2 = f32[16,16,4096]{2,1,0:T(8,128)} fusion(f32[16,16,4096]{2,1,0:T(8,128)} %param.31, s32[1024]{0:T(1024)S(1)} %pad_clamp_fusion.2), kind=kCustom, calls=%fused_computation.2 | custom fusion | bytes 8388672 | tf_op jit(solution)/shard_map/jit(_take)/gather | solution.py:95
  25.6 6.0 %all-to-all-start = ((bf16[8,2,3,4096]{3,1,2,0:T(2,128)(2,1)}), bf16[8,2,3,4096]{3,1,2,0:T(2,128)(2,1)S(1)}, u32[]{:S(2)}, u32[]{:S(2)}) async-start(bf16[8,2,3,4096]{3,1,2,0:T(2,128)(2,1)} %broadcast_select_fusion.2), calls=%async_computation | async-start | bytes 786432 | tf_op jit(solution)/shard_map/all_to_all | solution.py:118
  31.6 4.7 %broadcast_select_fusion.1 = f32[8,2,16,4096]{3,2,1,0:T(8,128)} fusion(f32[8,2,16,4096]{3,2,1,0:T(8,128)} %bitcast.76, pred[8,2]{1,0:T(8,128)(4,1)S(1)} %copy.96), kind=kLoop, calls=%fused_computation.16 | loop fusion | flops 1048576 | bytes 8388624 | tf_op jit(solution)/shard_map/jit(_take)/select_n | solution.py:95
  36.4 6.4 %all-to-all-done = bf16[8,2,3,4096]{3,1,2,0:T(2,128)(2,1)S(1)} async-done(((bf16[8,2,3,4096]{3,1,2,0:T(2,128)(2,1)}), bf16[8,2,3,4096]{3,1,2,0:T(2,128)(2,1)S(1)}, u32[]{:S(2)}, u32[]{:S(2)}) %all-to-all-start) | async-done | bytes 393248 | tf_op jit(solution)/shard_map/all_to_all | solution.py:118
  42.7 4.6 %all-to-all-start.1 = ((f32[8,2,16,4096]{3,2,1,0:T(8,128)}), f32[8,2,16,4096]{3,2,1,0:T(8,128)}, u32[]{:S(2)}, u32[]{:S(2)}) async-start(f32[8,2,16,4096]{3,2,1,0:T(8,128)} %broadcast_select_fusion.1), calls=%async_computation.1 | async-start | bytes 8388608 | tf_op jit(solution)/shard_map/all_to_all | solution.py:112
  47.3 0.1 reshape_squeeze.13
  47.4 0.1 broadcast_in_dim.160
  47.6 0.2 broadcast_in_dim.161
  47.8 21.8 %gather_fusion.5 = bf16[512,16,512]{2,1,0:T(8,128)(2,1)} fusion(bf16[256,16,512]{2,1,0:T(8,128)(2,1)} %param.45, s32[1024]{0:T(1024)S(1)} %pad_clamp_fusion), kind=kCustom, calls=%fused_computation.5 | custom fusion | bytes 16779264 | tf_op jit(solution)/shard_map/jit(_take)/gather | solution.py:110
  69.7 7.4 %broadcast_select_fusion = bf16[8,2,512,512]{3,2,1,0:T(8,128)(2,1)} fusion(bf16[8,2,512,512]{3,2,1,0:T(8,128)(2,1)} %bitcast.73, pred[8,2,512]{2,1,0:T(4,128)(4,1)S(1)} %copy.105), kind=kLoop, calls=%fused_computation.14 | loop fusion | flops 4194304 | bytes 16785408 | tf_op jit(solution)/shard_map/jit(_take)/select_n | solution.py:110
  77.1 0.0 copy-start.11
  77.1 0.0 copy-start.14
  77.2 62.0 %all-to-all-done.1 = f32[8,2,16,4096]{3,2,1,0:T(8,128)} async-done(((f32[8,2,16,4096]{3,2,1,0:T(8,128)}), f32[8,2,16,4096]{3,2,1,0:T(8,128)}, u32[]{:S(2)}, u32[]{:S(2)}) %all-to-all-start.1) | async-done | bytes 4194336 | tf_op jit(solution)/shard_map/all_to_all | solution.py:112
  139.1 5.0 %all-to-all-start.3 = ((bf16[8,2,512,512]{3,2,1,0:T(8,128)(2,1)}), bf16[8,2,512,512]{3,2,1,0:T(8,128)(2,1)}, u32[]{:S(2)}, u32[]{:S(2)}) async-start(bf16[8,2,512,512]{3,2,1,0:T(8,128)(2,1)} %broadcast_select_fusion), calls=%async_computation.3 | async-start | bytes 16777216 | tf_op jit(solution)/shard_map/all_to_all | solution.py:119
  144.1 0.0 copy-start.9
  144.1 0.2 all-reduce.2.cloned.1.call-start
  144.5 0.2 fusion.18
  144.7 0.1 copy.118
  144.7 0.6 copy.101
  145.4 0.5 broadcast.186
  145.9 0.7 reduce.3
  146.6 0.1 reshape.195
  146.7 0.7 gather_fusion.4
  147.4 0.1 iota_compare_fusion
  147.5 0.3 copy.99
  147.9 1.4 gather_fusion.1
  149.3 2.1 copy_select_fusion
  151.4 2.2 multiply_reduce_fusion.1
  153.6 4.3 %fusion.26 = f32[32,544]{1,0:T(8,128)} fusion(bf16[4096,544]{0,1:T(8,128)(2,1)} %param.34, f32[32,4096]{1,0:T(8,128)S(1)} %multiply_reduce_fusion.1, f32[4096]{0:T(1024)S(1)} %copy-done.9), kind=kOutput, calls=%fused_computation.85 | convolution fusion | flops 143392768 | bytes 5066752 | tf_op jit(solution)/shard_map/dot_general | solution.py:134
  157.9 0.0 all-reduce.2.cloned.1.call-update
  158.0 1.4 fusion.9
  159.3 1.5 copy.116
  160.8 28.2 %all-reduce.2.cloned.1.call-done = f32[32,544]{1,0:T(8,128)} async-done(((f32[32,544]{1,0:T(8,128)}), f32[32,544]{1,0:T(8,128)}) %all-reduce.2.cloned.1.call-update) | async-done | bytes 69648 | tf_op jit(solution)/shard_map/psum | solution.py:135
  188.9 1.0 multiply_reduce_fusion.4
  189.9 1.0 multiply_reduce_fusion.2
  190.9 0.9 fusion.23
  191.8 3.3 fusion.29
  195.2 6.7 %gather_fusion.3 = f32[32,16,4096]{2,1,0:T(8,128)} fusion(f32[16,16,4096]{2,1,0:T(8,128)} %bitcast.5, s32[1024]{0:T(1024)S(1)} %pad_clamp_fusion.1), kind=kCustom, calls=%fused_computation.3 | custom fusion | bytes 16777344 | tf_op jit(solution)/shard_map/jit(_take)/gather | solution.py:106
  201.9 10.6 %multiply_reduce_fusion = (f32[32,4096]{1,0:T(8,128)S(1)}, f32[32,16,4096]{2,1,0:T(8,128)}) fusion(f32[32,16]{1,0:T(8,128)S(1)} %get-tuple-element.36, f32[32,16]{1,0:T(8,128)S(1)} %get-tuple-element.35, f32[32,4096]{1,0:T(8,128)S(1)} %get-tuple-element.34, f32[32,16,4096]{2,1,0:T(8,128)} %param.30, f32[32,16,4096]{2,1,0:T(8,128)} %gather_fusion.3, ...), kind=kLoop, calls=%fused_computation.12 | loop fusion | flops 16646144 | bytes 27004992 | tf_op jit(solution)/shard_map/reduce_sum | solution.py:150
  212.5 1.0 fusion.12
  213.5 112.7 %all-to-all-done.3 = bf16[8,2,512,512]{3,2,1,0:T(8,128)(2,1)} async-done(((bf16[8,2,512,512]{3,2,1,0:T(8,128)(2,1)}), bf16[8,2,512,512]{3,2,1,0:T(8,128)(2,1)}, u32[]{:S(2)}, u32[]{:S(2)}) %all-to-all-start.3) | async-done | bytes 8388640 | tf_op jit(solution)/shard_map/all_to_all | solution.py:119
  326.1 10.6 %gather_fusion.6 = bf16[32,512,512]{2,1,0:T(8,128)(2,1)} fusion(bf16[16,512,512]{2,1,0:T(8,128)(2,1)} %bitcast.10, s32[1024]{0:T(1024)S(1)} %pad_clamp_fusion.1), kind=kCustom, calls=%fused_computation.6 | custom fusion | bytes 33554560 | tf_op jit(solution)/shard_map/jit(_take)/gather | solution.py:106
  336.7 17.5 %select_select_fusion = bf16[32,512,512]{2,1,0:T(8,128)(2,1)} fusion(bf16[32,512,512]{2,1,0:T(8,128)(2,1)} %param.44, bf16[32,512,512]{2,1,0:T(8,128)(2,1)} %gather_fusion.6, pred[32]{0:T(512)(128)(4,1)S(1)} %get-tuple-element.31, pred[32]{0:T(512)(128)(4,1)S(1)} %get-tuple-element.39), kind=kLoop, calls=%fused_computation.7 | loop fusion | flops 16777216 | bytes 50331712 | tf_op jit(solution)/shard_map/jit(_where)/select_n | solution.py:108
  354.1 22.5 %copy.106 = bf16[32,512,512]{1,2,0:T(8,128)(2,1)} copy(bf16[32,512,512]{2,1,0:T(8,128)(2,1)} %select_select_fusion) | data formatting | bytes 33554432 | tf_op jit(solution)/shard_map/jit(_where)/select_n | solution.py:108
  376.7 4.7 %fusion.30 = (f32[32,2,8]{2,1,0:T(2,128)S(1)}, f32[32,2,8,512]{3,2,1,0:T(8,128)S(1)}) fusion(bf16[32,2,8,128]{3,2,1,0:T(8,128)(2,1)S(1)} %bitcast.81, bf16[32,512,2,2,128]{1,4,3,2,0:T(8,128)(2,1)} %bitcast.74, pred[32,512]{1,0:T(8,128)(4,1)S(1)} %iota_compare_fusion), kind=kOutput, calls=%fused_computation.87 | convolution fusion | flops 67894784 | bytes 9586688 | tf_op jit(solution)/shard_map/nkgd,ntkd->nkgt/dot_general | solution.py:18
  381.4 0.1 copy.111
  381.5 0.4 convert_reduce_fusion
  381.9 0.1 copy.114
  382.0 0.1 copy.112
  382.0 0.1 copy.113
  382.1 0.1 copy.115
  382.2 5.7 %fusion.8 = bf16[32,2,8,128]{3,2,1,0:T(8,128)(2,1)S(1)} fusion(bf16[32,512,2,2,128]{1,4,3,2,0:T(8,128)(2,1)} %bitcast.75, f32[32,2,8]{2,1,0:T(2,128)S(1)} %copy.115, f32[32,2,128]{2,1,0:T(2,128)S(1)} %bitcast.84, f32[32,2,8]{2,1,0:T(2,128)S(1)} %copy.113, f32[32,2,8]{2,1,0:T(2,128)S(1)} %copy.112, f32[32,2,8,512]{3,2,1,0:T(8,128)S(1)} %get-tuple-element.41, ...), kind=kOutput, calls=%fused_computation.25 | convolution fusion | flops 68222976 | bytes 9625600 | tf_op jit(solution)/shard_map/nkgt,ntkd->nkgd/dot_general | solution.py:28
  387.9 0.7 copy.129
  (51 shorter events, 0.3 us)
Async XLA Ops:
  7.2 10.2 %copy-start = (bf16[16,3,4096]{2,0,1:T(8,128)(2,1)S(1)}, bf16[16,3,4096]{2,0,1:T(8,128)(2,1)}, u32[]{:S(2)}) copy-start(bf16[16,3,4096]{2,0,1:T(8,128)(2,1)} %param.29) | copy-start | bytes 1179652
  8.6 17.0 %all-to-all-start.2 = ((f32[8,1,2]{2,1,0:T(1,128)}), f32[8,1,2]{2,1,0:T(1,128)S(1)}, u32[]{:S(2)}, u32[]{:S(2)}) async-start(f32[8,1,2]{2,1,0:T(1,128)} %copy.103), calls=%async_computation.2 | async-start | bytes 8192 | tf_op jit(solution)/shard_map/all_to_all | solution.py:113
  25.6 17.1 %all-to-all-start = ((bf16[8,2,3,4096]{3,1,2,0:T(2,128)(2,1)}), bf16[8,2,3,4096]{3,1,2,0:T(2,128)(2,1)S(1)}, u32[]{:S(2)}, u32[]{:S(2)}) async-start(bf16[8,2,3,4096]{3,1,2,0:T(2,128)(2,1)} %broadcast_select_fusion.2), calls=%async_computation | async-start | bytes 786432 | tf_op jit(solution)/shard_map/all_to_all | solution.py:118
  31.6 15.7 %copy-start.7 = (s32[1,8,2,32]{3,2,1,0:T(2,128)S(1)}, s32[1,8,2,32]{3,2,1,0:T(2,128)}, u32[]{:S(2)}) copy-start(s32[1,8,2,32]{3,2,1,0:T(2,128)} %param.51) | copy-start | bytes 6148
  42.7 96.4 %all-to-all-start.1 = ((f32[8,2,16,4096]{3,2,1,0:T(8,128)}), f32[8,2,16,4096]{3,2,1,0:T(8,128)}, u32[]{:S(2)}, u32[]{:S(2)}) async-start(f32[8,2,16,4096]{3,2,1,0:T(8,128)} %broadcast_select_fusion.1), calls=%async_computation.1 | async-start | bytes 8388608 | tf_op jit(solution)/shard_map/all_to_all | solution.py:112
  77.1 67.2 %copy-start.5 = (bf16[32,2048]{1,0:T(8,128)(2,1)S(1)}, bf16[32,2048]{1,0:T(8,128)(2,1)}, u32[]{:S(2)}) copy-start(bf16[32,2048]{1,0:T(8,128)(2,1)} %param.42) | copy-start | bytes 393220
  77.1 67.3 %copy-start.8 = (bf16[32,512]{1,0:T(8,128)(2,1)S(1)}, bf16[32,512]{1,0:T(8,128)(2,1)}, u32[]{:S(2)}) copy-start(bf16[32,512]{1,0:T(8,128)(2,1)} %param.43) | copy-start | bytes 98308
  77.1 67.6 %copy-start.3 = (bf16[32,4096]{1,0:T(8,128)(2,1)S(1)}, bf16[32,4096]{1,0:T(8,128)(2,1)}, u32[]{:S(2)}) copy-start(bf16[32,4096]{1,0:T(8,128)(2,1)} %param.26) | copy-start | bytes 786436
  77.1 68.2 %copy-start.6 = (bf16[4,4096]{1,0:T(4,128)(2,1)S(1)}, bf16[4,4096]{1,0:T(4,128)(2,1)}, u32[]{:S(2)}) copy-start(bf16[4,4096]{1,0:T(4,128)(2,1)} %param.32) | copy-start | bytes 98308
  77.1 68.2 %copy-start.11 = (s32[32]{0:T(128)S(1)}, s32[32]{0:T(128)}, u32[]{:S(2)}) copy-start(s32[32]{0:T(128)} %param.47) | copy-start | bytes 388
  77.1 68.2 %copy-start.14 = (s32[32]{0:T(128)S(1)}, s32[32]{0:T(128)}, u32[]{:S(2)}) copy-start(s32[32]{0:T(128)} %param.48) | copy-start | bytes 388
  77.1 70.2 %copy-start.15 = (s32[32]{0:T(128)S(1)}, s32[32]{0:T(128)}, u32[]{:S(2)}) copy-start(s32[32]{0:T(128)} %param.46) | copy-start | bytes 388
  139.1 187.0 %all-to-all-start.3 = ((bf16[8,2,512,512]{3,2,1,0:T(8,128)(2,1)}), bf16[8,2,512,512]{3,2,1,0:T(8,128)(2,1)}, u32[]{:S(2)}, u32[]{:S(2)}) async-start(bf16[8,2,512,512]{3,2,1,0:T(8,128)(2,1)} %broadcast_select_fusion), calls=%async_computation.3 | async-start | bytes 16777216 | tf_op jit(solution)/shard_map/all_to_all | solution.py:119
  144.1 9.5 %copy-start.9 = (f32[4096]{0:T(1024)S(1)}, f32[4096]{0:T(1024)}, u32[]{:S(2)}) copy-start(f32[4096]{0:T(1024)} %param.33) | copy-start | bytes 49156
  144.1 44.8 %all-reduce.2.cloned.1.call-start = ((), (), s32[]{:S(2)}) async-start(), calls=%async_computation.4 | async-start | bytes 163840 | tf_op jit(solution)/shard_map/psum | solution.py:135
  147.8 43.1 %copy-start.12 = (f32[16]{0:T(128)S(1)}, f32[16]{0:T(128)}, u32[]{:S(2)}) copy-start(f32[16]{0:T(128)} %param.36) | copy-start | bytes 196
  147.8 43.1 %copy-start.13 = (f32[16]{0:T(128)S(1)}, f32[16]{0:T(128)}, u32[]{:S(2)}) copy-start(f32[16]{0:T(128)} %param.37) | copy-start | bytes 196
  147.8 43.9 %copy-start.16 = (f32[4096]{0:T(1024)S(1)}, f32[4096]{0:T(1024)}, u32[]{:S(2)}) copy-start(f32[4096]{0:T(1024)} %param.39) | copy-start | bytes 49156
  147.8 43.9 %copy-start.17 = (f32[512]{0:T(512)S(1)}, f32[512]{0:T(512)}, u32[]{:S(2)}) copy-start(f32[512]{0:T(512)} %param.35) | copy-start | bytes 6148
  195.1 6.7 %copy-start.2 = (f32[16,4096]{1,0:T(8,128)S(1)}, f32[16,4096]{1,0:T(8,128)}, u32[]{:S(2)}) copy-start(f32[16,4096]{1,0:T(8,128)} %param.40) | copy-start | bytes 786436
  201.9 10.6 %copy-start.4 = (bf16[32,4096]{1,0:T(8,128)(2,1)S(1)}, bf16[32,4096]{1,0:T(8,128)(2,1)}, u32[]{:S(2)}) copy-start(bf16[32,4096]{1,0:T(8,128)(2,1)} %param.27) | copy-start | bytes 786436
  201.9 10.6 %copy-start.10 = (f32[4096]{0:T(1024)S(1)}, f32[4096]{0:T(1024)}, u32[]{:S(2)}) copy-start(f32[4096]{0:T(1024)} %param.41) | copy-start | bytes 49156
  376.7 12.0 %copy-start.1 = (bf16[16,3,4096]{2,0,1:T(8,128)(2,1)S(1)}, bf16[16,3,4096]{2,0,1:T(8,128)(2,1)}, u32[]{:S(2)}) copy-start(bf16[16,3,4096]{2,0,1:T(8,128)(2,1)} %param.29) | copy-start | bytes 1179652
Sparse Core Ops, SparseCore 0:
  158.1 30.8 all-reduce.1
where the time goes:
time: 397 us; the launch traced here: 395 us
  waiting for transfers between devices  209 us (53%)
  local copies, waits for them, and re-layouts  77 us (19%)
  other arithmetic  53.5 us (13%)
  starting transfers between devices  23 us (6%)
  matrix products  18.3 us (5%)
  between operations  14.5 us (4%)
    all_to_all x1, waiting for transfers between devices, shards(): lax.all_to_all(page_send, 'rep', split_axis=0, concat_axis=0, tiled=True)  113 us
    all_to_all x1, waiting for transfers between devices, shards(): lax.all_to_all(ssm_send, 'rep', split_axis=0, concat_axis=0, tiled=True)  62 us
    psum x1, waiting for transfers between devices, shards(): proj = lax.psum(proj_part, 'tp')  28.2 us
    select_n x1, local copies, waits for them, and re-layouts, pick_rows(): return jnp.where(flag, picked, local_rows)  22.5 us
    gather x1, local copies, waits for them, and re-layouts, shards(): jnp.take(kv_pool, page_list, axis=0)  21.8 us
    select_n x2, other arithmetic, pick_rows(): return jnp.where(flag, picked, local_rows)  19.6 us
    gather x3, local copies, waits for them, and re-layouts, pick_rows(): picked = jnp.take(flat, where_from, axis=0)  18.7 us
    reduce_sum x1, other arithmetic, shards(): jnp.sum(read_out[:, :, None] * new_ssm, axis=1) + skip * signal  10.6 us
  transfers between devices with their start and end apart: 5, of which 4 were waited for; matrix products, arithmetic and copies ran while one was open for 21% of the time, Pallas kernels for 0%

commit v1 on v0

v1 whole, which is shorter than its diff:
```python
import functools
import math

import jax
import jax.numpy as jnp
from jax import lax
from jax.experimental import pallas as pl
from jax.experimental.pallas import tpu as pltpu
from jax.sharding import PartitionSpec as P

HD = 128
MESH = pl.DeviceIdType.MESH
VMEM_LIMIT = 48 * 1024 * 1024


def params(**kw):
    return pltpu.CompilerParams(vmem_limit_bytes=VMEM_LIMIT, **kw)


def whole(shape):
    return pl.BlockSpec(shape, lambda *_: (0,) * len(shape))


def attend_row(q, ctx, nkv, length):
    heads, width = q.shape
    kv_heads = nkv.shape[0] // 2
    groups = heads // kv_heads
    tokens = ctx.shape[0]
    scale = 1.0 / math.sqrt(width)

    def of_head(parts):
        row = lax.broadcasted_iota(jnp.int32, parts[0].shape, 0)
        out = parts[0]
        for k in range(1, kv_heads):
            out = jnp.where(row >= k * groups, parts[k], out)
        return out

    nkv = nkv.astype(jnp.float32)
    q32 = q.astype(jnp.float32)
    scores = of_head(
        [
            lax.dot_general(
                q,
                ctx[:, 2 * k * width : (2 * k + 1) * width],
                (((1,), (1,)), ((), ())),
                preferred_element_type=jnp.float32,
            )
            for k in range(kv_heads)
        ]
    ) * scale
    live = lax.broadcasted_iota(jnp.int32, (heads, tokens), 1) < length
    masked = jnp.where(live, scores, -1e30)
    top = jnp.max(masked, axis=1, keepdims=True)
    prob = jnp.where(live, jnp.exp(masked - top), 0.0).astype(jnp.bfloat16)
    total = jnp.sum(prob.astype(jnp.float32), axis=1, keepdims=True)
    mix = of_head(
        [
            jnp.dot(
                prob,
                ctx[:, (2 * k + 1) * width : (2 * k + 2) * width],
                preferred_element_type=jnp.float32,
            )
            for k in range(kv_heads)
        ]
    )
    new_key = of_head(
        [jnp.broadcast_to(nkv[2 * k : 2 * k + 1], (heads, width)) for k in range(kv_heads)]
    )
    new_value = of_head(
        [jnp.broadcast_to(nkv[2 * k + 1 : 2 * k + 2], (heads, width)) for k in range(kv_heads)]
    )
    new_score = jnp.sum(q32 * new_key, axis=1, keepdims=True) * scale
    peak = jnp.maximum(top, new_score)
    old_scale = jnp.exp(top - peak)
    new_scale = jnp.exp(new_score - peak)
    result = (mix * old_scale + new_scale * new_value) / (total * old_scale + new_scale)
    return result.astype(jnp.bfloat16)


def resident_kernel(lens, q_ref, kv_ref, nkv_ref, out_ref):
    batch = q_ref.shape[0]
    base = pl.program_id(0) * batch
    rows = [attend_row(q_ref[i], kv_ref[i], nkv_ref[i], lens[base + i]) for i in range(batch)]
    for i in range(batch):
        out_ref[i] = rows[i]


def paged_kernel(lens, pages, q_ref, pool_ref, nkv_ref, out_ref, ctx_ref):
    batch = q_ref.shape[0]
    base = pl.program_id(0) * batch
    page = pool_ref.shape[1]
    page_count = ctx_ref.shape[1] // page
    for i in range(batch):
        for j in range(page_count):
            ctx_ref[i, j * page : (j + 1) * page, :] = pool_ref[pages[(base + i) * page_count + j]]
    rows = [attend_row(q_ref[i], ctx_ref[i], nkv_ref[i], lens[base + i]) for i in range(batch)]
    for i in range(batch):
        out_ref[i] = rows[i]


def attend_resident(q, kv, nkv, lens):
    rows, heads, width = q.shape
    tokens, kv_width = kv.shape[1:]
    batch = 4
    return pl.pallas_call(
        resident_kernel,
        grid_spec=pltpu.PrefetchScalarGridSpec(
            num_scalar_prefetch=1,
            grid=(rows // batch,),
            in_specs=[
                pl.BlockSpec((batch, heads, width), lambda i, *_: (i, 0, 0)),
                pl.BlockSpec((batch, tokens, kv_width), lambda i, *_: (i, 0, 0)),
                pl.BlockSpec((batch,) + nkv.shape[1:], lambda i, *_: (i, 0, 0)),
            ],
            out_specs=pl.BlockSpec((batch, heads, width), lambda i, *_: (i, 0, 0)),
        ),
        out_shape=jax.ShapeDtypeStruct(q.shape, jnp.bfloat16),
        compiler_params=params(),
        cost_estimate=pl.CostEstimate(
            flops=rows * tokens * heads * width * 8,
            bytes_accessed=2 * kv.size,
            transcendentals=rows * heads * tokens,
        ),
        name="attend_resident",
    )(lens, q, kv, nkv)


def attend_paged(q, pool, nkv, lens, pages, tokens):
    entries, heads, width = q.shape
    batch = 4
    return pl.pallas_call(
        paged_kernel,
        grid_spec=pltpu.PrefetchScalarGridSpec(
            num_scalar_prefetch=2,
            grid=(entries // batch,),
            in_specs=[
                pl.BlockSpec((batch, heads, width), lambda i, *_: (i, 0, 0)),
                whole(pool.shape),
                pl.BlockSpec((batch,) + nkv.shape[1:], lambda i, *_: (i, 0, 0)),
            ],
            out_specs=pl.BlockSpec((batch, heads, width), lambda i, *_: (i, 0, 0)),
            scratch_shapes=[pltpu.VMEM((batch, tokens, pool.shape[2]), jnp.bfloat16)],
        ),
        out_shape=jax.ShapeDtypeStruct(q.shape, jnp.bfloat16),
        compiler_params=params(),
        cost_estimate=pl.CostEstimate(
            flops=entries * tokens * heads * width * 8,
            bytes_accessed=2 * pool.size,
            transcendentals=entries * heads * tokens,
        ),
        name="attend_paged",
    )(lens, pages, q, pool, nkv)


def pack_kernel(slots, pool_ref, out_ref):
    out_ref[...] = pool_ref[...].astype(jnp.bfloat16)


def pack_states(pool, slots):
    entries = slots.shape[0]
    block = (1,) + pool.shape[1:]
    return pl.pallas_call(
        pack_kernel,
        grid_spec=pltpu.PrefetchScalarGridSpec(
            num_scalar_prefetch=1,
            grid=(entries,),
            in_specs=[pl.BlockSpec(block, lambda i, slots: (slots[i], 0, 0))],
            out_specs=pl.BlockSpec(block, lambda i, slots: (i, 0, 0)),
        ),
        out_shape=jax.ShapeDtypeStruct((entries,) + pool.shape[1:], jnp.bfloat16),
        compiler_params=params(),
        cost_estimate=pl.CostEstimate(
            flops=0, bytes_accessed=6 * entries * pool[0].size, transcendentals=0
        ),
        name="pack_states",
    )(slots, pool)


def conv_kernel(source, x_ref, state_ref, got_ref, weight_ref, bias_ref, proj_ref,
                mixed_ref, conv_ref, part_ref, sum_ref):
    rows, taps = state_ref.shape[:2]
    weight = weight_ref[...].astype(jnp.float32)
    for r in range(rows):
        entry = source[r]
        prev = jnp.where(
            entry >= 0,
            got_ref[jnp.maximum(entry, 0)].astype(jnp.float32)[:taps],
            state_ref[r].astype(jnp.float32),
        )
        new = x_ref[r : r + 1, :].astype(jnp.float32)
        conv_ref[r] = jnp.concatenate([prev[1:], new], axis=0).astype(jnp.bfloat16)
        sum_ref[r : r + 1, :] = (
            jnp.sum(prev * weight[:taps], axis=0, keepdims=True) + new * weight[taps:]
        )
    total = sum_ref[...] + bias_ref[...]
    mixed = (total / (1.0 + jnp.exp(-total))).astype(jnp.bfloat16)
    mixed_ref[...] = mixed.astype(jnp.float32)
    part_ref[...] = jnp.dot(mixed, proj_ref[...], preferred_element_type=jnp.float32)


def convolve(source, x_in, state, got, weight, bias, x_proj):
    rows, channels = x_in.shape
    outs = (
        jax.ShapeDtypeStruct((rows, channels), jnp.float32),
        jax.ShapeDtypeStruct(state.shape, jnp.bfloat16),
        jax.ShapeDtypeStruct((rows, x_proj.shape[1]), jnp.float32),
    )
    operands = (x_in, state, got, weight, bias, x_proj)
    return pl.pallas_call(
        conv_kernel,
        grid_spec=pltpu.PrefetchScalarGridSpec(
            num_scalar_prefetch=1,
            grid=(1,),
            in_specs=[whole(a.shape) for a in operands],
            out_specs=[whole(o.shape) for o in outs],
            scratch_shapes=[pltpu.VMEM((rows, channels), jnp.float32)],
        ),
        out_shape=outs,
        compiler_params=params(),
        cost_estimate=pl.CostEstimate(
            flops=2 * rows * x_proj.size, bytes_accessed=2 * x_proj.size + 8 * x_in.size * 2,
            transcendentals=x_in.size,
        ),
        name="conv_proj",
    )(source, *operands)


def step_kernel(count, part_ref, dt_proj_ref, bias_ref, dt_gain_ref, b_gain_ref, c_gain_ref,
                dt_ref, bc_ref, got_ref, send_sem, recv_sem):
    me = lax.axis_index("tp")
    barrier = pltpu.get_barrier_semaphore()
    for k in range(1, count):
        pl.semaphore_signal(
            barrier, inc=1, device_id={"tp": lax.rem(me + k, count)}, device_id_type=MESH
        )
    pl.semaphore_wait(barrier, count - 1)
    copies = []
    for k in range(1, count):
        copy = pltpu.make_async_remote_copy(
            src_ref=part_ref,
            dst_ref=got_ref.at[k - 1],
            send_sem=send_sem.at[k - 1],
            recv_sem=recv_sem.at[k - 1],
            device_id={"tp": lax.rem(me + k, count)},
            device_id_type=MESH,
        )
        copy.start()
        copies.append(copy)
    proj = part_ref[...]
    for k, copy in enumerate(copies):
        copy.wait_recv()
        proj = proj + got_ref[k]
    rank = dt_proj_ref.shape[0]
    states = b_gain_ref.shape[1]

    def rms_scaled(values, gain):
        mean = jnp.mean(values * values, axis=-1, keepdims=True)
        return (values * lax.rsqrt(mean + 1e-06) * gain).astype(jnp.bfloat16)

    normed = rms_scaled(proj[:, :rank], dt_gain_ref[...])
    raw = jnp.dot(normed, dt_proj_ref[...], preferred_element_type=jnp.float32) + bias_ref[...]
    dt_ref[...] = jnp.maximum(raw, 0.0) + jnp.log1p(jnp.exp(-jnp.abs(raw)))
    bc_ref[0] = rms_scaled(proj[:, rank : rank + states], b_gain_ref[...]).astype(jnp.float32)
    bc_ref[1] = rms_scaled(proj[:, rank + states :], c_gain_ref[...]).astype(jnp.float32)
    for copy in copies:
        copy.wait_send()


def step_sizes(count, part, dt_proj, dt_bias, dt_gain, b_gain, c_gain):
    rows = part.shape[0]
    channels = dt_proj.shape[1]
    vmem = pl.BlockSpec(memory_space=pltpu.VMEM)
    return pl.pallas_call(
        functools.partial(step_kernel, count),
        out_shape=(
            jax.ShapeDtypeStruct((rows, channels), jnp.float32),
            jax.ShapeDtypeStruct((2, rows, b_gain.shape[1]), jnp.float32),
        ),
        in_specs=[vmem] * 6,
        out_specs=(vmem, vmem),
        scratch_shapes=[
            pltpu.VMEM((count - 1,) + part.shape, jnp.float32),
            pltpu.SemaphoreType.DMA((count - 1,)),
            pltpu.SemaphoreType.DMA((count - 1,)),
        ],
        compiler_params=params(collective_id=0, has_side_effects=True),
        cost_estimate=pl.CostEstimate(
            flops=2 * rows * dt_proj.size, bytes_accessed=2 * dt_proj.size + 4 * rows * channels,
            transcendentals=2 * rows * channels,
        ),
        name="tp_sum_step",
    )(part, dt_proj, dt_bias, dt_gain, b_gain, c_gain)


def update_row(row, prev, dt_ref, signal_ref, bc_ref, decay_ref):
    states = decay_ref.shape[0]
    eye = lax.broadcasted_iota(jnp.int32, (states, states), 0) == lax.broadcasted_iota(
        jnp.int32, (states, states), 1
    )

    def column(which):
        line = bc_ref[which, pl.ds(row, 1), :]
        spread = jnp.where(eye, jnp.broadcast_to(line, (states, states)), 0.0)
        return jnp.sum(spread, axis=1, keepdims=True)

    dt = dt_ref[pl.ds(row, 1), :]
    drive = dt * signal_ref[pl.ds(row, 1), :]
    new = jnp.exp(-dt * decay_ref[...]) * prev + drive * column(0)
    return new, jnp.sum(column(1) * new, axis=0, keepdims=True)


def early_kernel(perm, state_ref, dt_ref, signal_ref, bc_ref, decay_ref, new_ref, y_ref, *, first):
    step = pl.program_id(0)

    @pl.when(step == 0)
    def _():
        y_ref[...] = jnp.zeros_like(y_ref)

    row = perm[first + step]
    new, y = update_row(row, state_ref[0], dt_ref, signal_ref, bc_ref, decay_ref)
    new_ref[0] = new
    y_ref[pl.ds(row, 1), :] = y


def late_kernel(perm, source, state_ref, got_ref, dt_ref, signal_ref, bc_ref, decay_ref, early_y,
                skip_ref, z_ref, kept_ref, new_ref, out_ref, y_ref):
    step = pl.program_id(0)

    @pl.when(step == 0)
    def _():
        y_ref[...] = early_y[...]

    row = perm[step]
    prev = jnp.where(source[row] >= 0, got_ref[0].astype(jnp.float32), state_ref[0])
    new, y = update_row(row, prev, dt_ref, signal_ref, bc_ref, decay_ref)
    new_ref[0] = new
    y_ref[pl.ds(row, 1), :] = y

    @pl.when(step == pl.num_programs(0) - 1)
    def _():
        z = z_ref[...].astype(jnp.float32)
        gate = z / (1.0 + jnp.exp(-z))
        out_ref[...] = ((y_ref[...] + skip_ref[...] * signal_ref[...]) * gate).astype(jnp.bfloat16)


def update_early(perm, state, dt, signal, bc, decay, late):
    rows = state.shape[0]
    block = (1,) + state.shape[1:]
    shared = (dt, signal, bc, decay)
    return pl.pallas_call(
        functools.partial(early_kernel, first=late),
        grid_spec=pltpu.PrefetchScalarGridSpec(
            num_scalar_prefetch=1,
            grid=(rows - late,),
            in_specs=[pl.BlockSpec(block, lambda i, perm: (perm[late + i], 0, 0))]
            + [whole(a.shape) for a in shared],
            out_specs=[
                pl.BlockSpec(block, lambda i, perm: (perm[late + i], 0, 0)),
                whole(dt.shape),
            ],
        ),
        out_shape=(
            jax.ShapeDtypeStruct(state.shape, jnp.float32),
            jax.ShapeDtypeStruct(dt.shape, jnp.float32),
        ),
        compiler_params=params(),
        cost_estimate=pl.CostEstimate(
            flops=8 * (rows - late) * state[0].size,
            bytes_accessed=8 * (rows - late) * state[0].size,
            transcendentals=(rows - late) * state[0].size,
        ),
        name="ssm_early",
    )(perm, state, *shared)


def update_late(perm, source, state, got, dt, signal, bc, decay, early_y, skip, z, kept, late):
    block = (1,) + state.shape[1:]
    shared = (dt, signal, bc, decay, early_y, skip, z)
    return pl.pallas_call(
        late_kernel,
        grid_spec=pltpu.PrefetchScalarGridSpec(
            num_scalar_prefetch=2,
            grid=(late,),
            in_specs=[
                pl.BlockSpec(block, lambda i, perm, source: (perm[i], 0, 0)),
                pl.BlockSpec(
                    block, lambda i, perm, source: (jnp.maximum(source[perm[i]], 0), 0, 0)
                ),
            ]
            + [whole(a.shape) for a in shared]
            + [pl.BlockSpec(memory_space=pl.ANY)],
            out_specs=[
                pl.BlockSpec(block, lambda i, perm, source: (perm[i], 0, 0)),
                whole(dt.shape),
            ],
            scratch_shapes=[pltpu.VMEM(dt.shape, jnp.float32)],
        ),
        out_shape=(
            jax.ShapeDtypeStruct(state.shape, jnp.float32),
            jax.ShapeDtypeStruct(dt.shape, jnp.bfloat16),
        ),
        input_output_aliases={4 + len(shared): 0},
        compiler_params=params(),
        cost_estimate=pl.CostEstimate(
            flops=8 * late * state[0].size,
            bytes_accessed=10 * late * state[0].size,
            transcendentals=late * state[0].size,
        ),
        name="ssm_late",
    )(perm, source, state, got, *shared, kept)


def shards(
    x_in,
    z_gate,
    conv_state,
    conv_pool,
    ssm_state,
    ssm_pool,
    conv_weight,
    conv_bias,
    x_proj,
    dt_gain,
    b_gain,
    c_gain,
    dt_proj,
    dt_bias,
    decay_rate,
    skip,
    query,
    new_kv,
    kv_cache,
    kv_pool,
    ctx_len,
    row_owner,
    row_pos,
    swap_slot,
    swap_lens,
    swap_pages,
):
    peer_count = lax.axis_size("rep")
    tp_count = lax.axis_size("tp")
    row_count, channels = x_in.shape
    slot_cap = swap_slot.shape[2]
    entry_count = peer_count * slot_cap
    taps = conv_state.shape[1]
    head_count = query.shape[1] // HD
    slot_list = swap_slot[0].reshape(-1)
    resumed = row_owner >= 0
    source = jnp.where(resumed, row_owner * slot_cap + row_pos, -1).astype(jnp.int32)
    row_ids = jnp.arange(row_count, dtype=jnp.int32)
    entry_ids = jnp.arange(entry_count, dtype=jnp.int32)
    match = source[None, :] == entry_ids[:, None]
    entry_row = jnp.sum(jnp.where(match, row_ids[None, :], 0), axis=1)
    before = row_ids[None, :] < row_ids[:, None]
    earlier = jnp.sum((before & (resumed[None, :] == resumed[:, None])).astype(jnp.int32), axis=1)
    place = jnp.where(resumed, earlier, earlier + jnp.sum(resumed.astype(jnp.int32)))
    perm = jnp.sum(
        jnp.where(place[None, :] == row_ids[:, None], row_ids[None, :], 0), axis=1
    ).astype(jnp.int32)

    def exchange(block):
        split = block.reshape((peer_count, slot_cap) + block.shape[1:])
        out = lax.all_to_all(split, "rep", split_axis=0, concat_axis=0, tiled=True)
        return out.reshape(block.shape)

    asked = jnp.take(jnp.concatenate([query, new_kv], axis=1), entry_row, axis=0, mode="clip")
    asked = jnp.pad(asked, ((0, 0), (0, channels - asked.shape[1])))
    taps_out = jnp.take(conv_pool, slot_list, axis=0, mode="clip")
    first = exchange(jnp.concatenate([taps_out, asked[:, None, :]], axis=1))

    states = pack_states(ssm_pool, slot_list)
    first, states = lax.optimization_barrier((first, states))
    states_in = exchange(states)

    query_rows = query.reshape(row_count, head_count, HD)
    new_rows = new_kv.reshape(row_count, -1, HD)
    attn_here = attend_resident(query_rows, kv_cache, new_rows, ctx_len).reshape(query.shape)

    mixed, new_conv, part = convolve(
        source, x_in, conv_state, first, conv_weight, conv_bias[None, :], x_proj
    )
    dt_step, bc = step_sizes(
        tp_count, part, dt_proj, dt_bias[None, :], dt_gain[None, :], b_gain[None, :],
        c_gain[None, :],
    )

    query_width = query.shape[1]
    asked_in = first[:, taps, :]
    query_in = asked_in[:, :query_width].reshape(entry_count, head_count, HD)
    new_in = asked_in[:, query_width : query_width + new_kv.shape[1]].reshape(entry_count, -1, HD)
    attn_there = attend_paged(
        query_in, kv_pool, new_in, swap_lens[0].reshape(-1), swap_pages[0].reshape(-1),
        kv_cache.shape[1],
    ).reshape(entry_count, query_width)
    attn_back = exchange(attn_there)
    picked = jnp.take(attn_back, jnp.maximum(source, 0), axis=0, mode="clip")
    attn_out = jnp.where(resumed[:, None], picked, attn_here)

    late = min(row_count, entry_count)
    if late < row_count:
        kept, early_y = update_early(perm, ssm_state, dt_step, mixed, bc, decay_rate, late)
    else:
        kept, early_y = jnp.zeros_like(ssm_state), jnp.zeros_like(dt_step)
    new_ssm, mamba_out = update_late(
        perm, source, ssm_state, states_in, dt_step, mixed, bc, decay_rate, early_y,
        skip[None, :], z_gate, kept, late,
    )
    return (mamba_out, attn_out, new_ssm, new_conv)


def solution(mesh):
    in_specs = (
        P("rep", "tp"),
        P("rep", "tp"),
        P("rep", None, "tp"),
        P("rep", None, "tp"),
        P("rep", None, "tp"),
        P("rep", None, "tp"),
        P(None, "tp"),
        P("tp"),
        P("tp", None),
        P(),
        P(),
        P(),
        P(None, "tp"),
        P("tp"),
        P(None, "tp"),
        P("tp"),
        P("rep", "tp"),
        P("rep", "tp"),
        P("rep", None, "tp"),
        P("rep", None, "tp"),
        P("rep"),
        P("rep"),
        P("rep"),
        P("rep", None, None),
        P("rep", None, None),
        P("rep", None, None, None),
    )
    out_specs = (P("rep", "tp"), P("rep", "tp"), P("rep", None, "tp"), P("rep", None, "tp"))
    return jax.shard_map(shards, mesh=mesh, in_specs=in_specs, out_specs=out_specs, check_vma=False)
```

time: 397 us -> 123 us (0.31)
  waiting for transfers between devices: 209 us -> 3.87 us
  Pallas kernels: 0 us -> 65.8 us
  local copies, waits for them, and re-layouts: 77 us -> 23.2 us
  other arithmetic: 53.5 us -> 5.46 us
  matrix products: 18.3 us -> 0 us
  between operations: 14.5 us -> 1.11 us
  starting transfers between devices: 23 us -> 10.9 us
  blocking collectives: 0 us -> 10.4 us
    all_to_all x4 -> x2, waiting for transfers between devices: 181 us -> 3.87 us  [exchange(): out = lax.all_to_all(split, 'rep', split_axis=0, concat_axis=0, tiled=True)]
    pallas_call x0 -> x7, Pallas kernels: none -> 65.8 us  [the longest x1 13.5 us: attend_resident(): pl.pallas_call(resident_kernel, grid_spec=pltpu.PrefetchScalarGridSpec(nu...]
    gather x8 -> x3, local copies, waits for them, and re-layouts: 48.2 us -> 2.94 us  [the longest x1 1.69 us: shards(): taps_out = jnp.take(conv_pool, slot_list, axis=0, mode='clip')]
    select_n x8 -> x2, other arithmetic: 32.9 us -> 1.39 us  [the longest x1 0.74 us: shards(): attn_out = jnp.where(resumed[:, None], picked, attn_here)]
    psum x1 -> x0, waiting for transfers between devices: 28.2 us -> none  [shards(): proj = lax.psum(proj_part, 'tp')]
    select_n x1 -> x0, local copies, waits for them, and re-layouts: 22.5 us -> none  [pick_rows(): return jnp.where(flag, picked, local_rows)]
    dot_general x5 -> x0, matrix products: 18.3 us -> none  [the longest x1 5.71 us: attend_block(): jnp.einsum('nkgt,ntkd->nkgd', prob_weights, value_rows, preferred_element...]
    unnamed x40 -> x75, local copies, waits for them, and re-layouts: 3.03 us -> 19.1 us
  transfers between devices with their start and end apart: 5 -> 2, of which waited for: 4 -> 1; matrix products, arithmetic and copies ran while one was open for 21% -> 11% of each run, Pallas kernels for 0% -> 40%
where the time goes in v1:
time: 123 us; the launch traced here: 121 us
  Pallas kernels  65.8 us (53%)
  local copies, waits for them, and re-layouts  23.2 us (19%)
  starting transfers between devices  10.9 us (9%)
  blocking collectives  10.4 us (8%)
  other arithmetic  5.46 us (4%)
  waiting for transfers between devices  3.87 us (3%)
    unnamed x75, local copies, waits for them, and re-layouts  19.1 us
    pallas_call x1, Pallas kernels, attend_resident(): pl.pallas_call(resident_kernel, grid_spec=pltpu.PrefetchScalarGridSpec(nu...  13.5 us
    pallas_call x1, Pallas kernels, update_late(): pl.pallas_call(late_kernel, grid_spec=pltpu.PrefetchScalarGridSpec(num_sc...  12 us
    pallas_call x1, Pallas kernels, update_early(): pl.pallas_call(functools.partial(early_kernel, first=late), grid_spec=plt...  11.3 us
    all_to_all x2, starting transfers between devices, exchange(): out = lax.all_to_all(split, 'rep', split_axis=0, concat_axis=0, tiled=True)  10.9 us
    all_to_all x1, blocking collectives, exchange(): out = lax.all_to_all(split, 'rep', split_axis=0, concat_axis=0, tiled=True)  10.4 us
    pallas_call x1, Pallas kernels, pack_states(): pl.pallas_call(pack_kernel, grid_spec=pltpu.PrefetchScalarGridSpec(num_sc...  10.4 us
    pallas_call x1, Pallas kernels, convolve(): pl.pallas_call(conv_kernel, grid_spec=pltpu.PrefetchScalarGridSpec(num_sc...  6.56 us
  transfers between devices with their start and end apart: 2, of which 1 were waited for; matrix products, arithmetic and copies ran while one was open for 11% of the time, Pallas kernels for 40%

profile of v1, /device:TPU:0, one launch (start us, length us, event | category | flops | bytes accessed | tf_op | source)
XLA Modules:
  0.0 120.8 jit_solution(10574541047292876893)
XLA Ops:
  0.6 0.0 copy-start
  0.6 1.4 %broadcast_maximum_fusion = (s32[32]{0:T(128)S(1)}, s32[32]{0:T(128)S(1)}, s32[]{:T(128)}) fusion(s32[32]{0:T(128)} %param.48, s32[32]{0:T(128)} %param.47), kind=kLoop, calls=%fused_computation.21 | loop fusion | flops 223 | bytes 516 | tf_op jit(solution)/shard_map/max | solution.py:497
  2.0 0.1 select_reduce_fusion.1
  2.1 0.8 copy.45
  2.9 0.1 reshape.55.slots
  3.0 0.9 pad_maximum_fusion.1
  3.9 0.6 gather_fusion.1
  4.5 0.0 copy-start.30
  4.5 0.0 copy-start.32
  4.6 0.2 concatenate.15
  4.8 1.7 %gather_fusion = bf16[16,3,4096]{2,0,1:T(8,128)(2,1)S(1)} fusion(bf16[16,3,4096]{2,0,1:T(8,128)(2,1)S(1)} %copy-done, s32[1024]{0:T(1024)S(1)} %pad_clamp_fusion.2), kind=kCustom, calls=%fused_computation | custom fusion | bytes 786496 | tf_op jit(solution)/shard_map/jit(_take)/gather | solution.py:469
  6.5 0.3 copy.52
  6.8 1.3 %pad_maximum_fusion = bf16[8,2,4,4096]{3,2,1,0:T(4,128)(2,1)} fusion(bf16[8,2,1,4096]{3,2,1,0:T(2,128)(2,1)S(1)} %concatenate.15, bf16[8,2,3,4096]{3,2,1,0:T(4,128)(2,1)S(1)} %bitcast.33), kind=kLoop, calls=%fused_computation.3 | loop fusion | flops 1048576 | bytes 1048576 | tf_op jit(solution)/shard_map/concatenate | solution.py:470
  8.2 7.3 %all-to-all-start = ((bf16[8,2,4,4096]{3,2,1,0:T(4,128)(2,1)}), bf16[8,2,4,4096]{3,2,1,0:T(4,128)(2,1)S(1)}, u32[]{:S(2)}, u32[]{:S(2)}) async-start(bf16[8,2,4,4096]{3,2,1,0:T(4,128)(2,1)} %pad_maximum_fusion), calls=%async_computation | async-start | bytes 1048576 | tf_op jit(solution)/shard_map/all_to_all | solution.py:464
  15.4 0.1 reshape_squeeze.11.pages
  15.5 0.1 copy.50
  15.6 0.1 reshape_squeeze.10.lens
  15.7 10.4 %pack_states.1 = bf16[16,16,4096]{2,1,0:T(8,128)(2,1)} custom-call(s32[16]{0:T(128)S(1)} %reshape.55.slots, f32[16,16,4096]{2,1,0:T(8,128)} %pool_ref.2), custom_call_target="tpu_custom_call" | custom-call | bytes 6291456 | tf_op jit(solution)/shard_map/pack_states/pallas_call | solution.py:162
  26.1 3.9 %all-to-all-done = bf16[8,2,4,4096]{3,2,1,0:T(4,128)(2,1)S(1)} async-done(((bf16[8,2,4,4096]{3,2,1,0:T(4,128)(2,1)}), bf16[8,2,4,4096]{3,2,1,0:T(4,128)(2,1)S(1)}, u32[]{:S(2)}, u32[]{:S(2)}) %all-to-all-start) | async-done | bytes 524320 | tf_op jit(solution)/shard_map/all_to_all | solution.py:464
  29.9 0.3 slice.9
  30.2 0.2 copy.59
  30.4 0.0 copy-start.29
  30.4 0.0 copy-start.27
  30.5 0.0 copy-start.2
  30.5 2.2 %copy-done.2 = bf16[256,16,512]{2,1,0:T(8,128)(2,1)S(1)} copy-done((bf16[256,16,512]{2,1,0:T(8,128)(2,1)S(1)}, bf16[256,16,512]{2,1,0:T(8,128)(2,1)}, u32[]{:S(2)}) %copy-start.2) | copy-done | bytes 4194328
  32.7 5.7 %attend_paged.1 = bf16[16,16,128]{2,1,0:T(8,128)(2,1)S(1)} custom-call(s32[16]{0:T(128)S(1)} %reshape_squeeze.10.lens, s32[512]{0:T(512)S(1)} %reshape_squeeze.11.pages, bf16[16,16,128]{2,1,0:T(8,128)(2,1)S(1)} %bitcast.26, bf16[256,16,512]{2,1,0:T(8,128)(2,1)S(1)} %copy-done.2, bf16[16,4,128]{2,1,0:T(4,128)(2,1)S(1)} %reshape.48.nkv_ref), custom_call_target="tpu_custom_call" | custom-call | flops 134217728 | bytes 4194304 | tf_op jit(solution)/shard_map/attend_paged/pallas_call | solution.py:131
  38.5 10.4 %all_to_all.15 = bf16[8,2,2048]{2,1,0:T(2,128)(2,1)} all-to-all(bf16[8,2,2048]{2,1,0:T(2,128)(2,1)S(1)} %reshape_reshape.3), channel_id=1, replica_groups=mesh['rep'=8,'tp'=4] {'rep'}, dimensions={0} | all-to-all | bytes 131072 | tf_op jit(solution)/shard_map/all_to_all | solution.py:464
  48.9 0.0 copy-done.4
  48.9 3.6 %all-to-all-start.1 = ((bf16[8,2,16,4096]{3,2,1,0:T(8,128)(2,1)}), bf16[8,2,16,4096]{3,2,1,0:T(8,128)(2,1)S(1)}, u32[]{:S(2)}, u32[]{:S(2)}) async-start(bf16[8,2,16,4096]{3,2,1,0:T(8,128)(2,1)} %bitcast.2), calls=%async_computation.1 | async-start | bytes 4194304 | tf_op jit(solution)/shard_map/all_to_all | solution.py:464
  52.5 0.0 copy-done.29
  52.6 1.8 %copy.48.state_ref = bf16[32,3,4096]{2,1,0:T(4,128)(2,1)S(1)} copy(bf16[32,3,4096]{2,0,1:T(8,128)(2,1)} %param.28) | data formatting | bytes 1572864 | tf_op args[2]
  54.4 0.0 copy-start.24
  54.4 7.5 %copy.49.proj_ref = bf16[4096,544]{1,0:T(8,128)(2,1)} copy(bf16[4096,544]{0,1:T(8,128)(2,1)} %param.34) | data formatting | bytes 8912896 | tf_op args[8]
  62.0 0.0 copy-done.24
  62.0 0.0 copy-start.12
  62.0 0.0 copy-start.15
  62.0 0.0 copy-start.16
  62.0 13.5 %attend_resident.1 = bf16[32,16,128]{2,1,0:T(8,128)(2,1)S(1)} custom-call(s32[32]{0:T(128)S(1)} %copy-done.24, bf16[32,16,128]{2,1,0:T(8,128)(2,1)S(1)} %bitcast.25, bf16[32,512,512]{2,1,0:T(8,128)(2,1)} %kv_ref.1, bf16[32,4,128]{2,1,0:T(4,128)(2,1)S(1)} %reshape.51.nkv_ref), custom_call_target="tpu_custom_call" | custom-call | flops 268435456 | bytes 16777216 | tf_op jit(solution)/shard_map/attend_resident/pallas_call | solution.py:105
  75.6 0.2 convert_reduce_fusion
  75.8 0.7 add_select_fusion
  76.4 0.1 select_reduce_fusion.perm
  76.6 0.0 copy-start.3
  76.6 0.0 copy-start.17
  76.6 0.0 copy-start.23
  76.6 0.0 copy-start.25
  76.6 0.0 copy-start.26
  76.7 6.6 %conv_proj.1 = (f32[32,4096]{1,0:T(8,128)S(1)}, bf16[32,3,4096]{2,1,0:T(4,128)(2,1)S(1)}, f32[32,544]{1,0:T(8,128)S(1)}) custom-call(s32[32]{0:T(128)S(1)} %get-tuple-element.39.source, bf16[32,4096]{1,0:T(8,128)(2,1)S(1)} %copy-done.12, bf16[32,3,4096]{2,1,0:T(4,128)(2,1)S(1)} %copy.48.state_ref, bf16[16,4,4096]{2,1,0:T(4,128)(2,1)S(1)} %bitcast.23, ...), custom_call_target="tpu_custom_call" | custom-call | flops 142606336 | bytes 6553600 | tf_op jit(solution)/shard_map/conv_proj/pallas_call | solution.py:209
  83.2 0.0 copy-start.8
  83.3 1.5 %copy.51 = bf16[32,3,4096]{2,0,1:T(8,128)(2,1)} copy(bf16[32,3,4096]{2,1,0:T(4,128)(2,1)S(1)} %get-tuple-element.37) | data formatting | bytes 1572864
  84.7 6.3 %tp_sum_step.1 = (f32[32,4096]{1,0:T(8,128)S(1)}, f32[2,32,16]{2,1,0:T(8,128)S(1)}) custom-call(f32[32,544]{1,0:T(8,128)S(1)} %get-tuple-element.17.part_ref, bf16[512,4096]{1,0:T(8,128)(2,1)S(1)} %copy-done.3, f32[1,4096]{1,0:T(1,128)S(1)} %bitcast.28, f32[1,512]{1,0:T(1,128)S(1)} %bitcast.30, f32[1,16]{1,0:T(1,128)S(1)} %bitcast.31, f32[1,16]{1,0:T(1,128)S(1)} %bitcast.32), custom_call_target="tpu_custom_call" | custom-call | flops 134217728 | bytes 4718592 | tf_op jit(solution)/shard_map/tp_sum_step/pallas_call | solution.py:273
  91.1 0.0 copy-start.13
  91.1 0.0 copy-start.11
  91.1 0.0 copy-start.18
  91.1 11.3 %ssm_early.1 = (f32[32,16,4096]{2,1,0:T(8,128)}, f32[32,4096]{1,0:T(8,128)S(1)}) custom-call(s32[32]{0:T(128)S(1)} %select_reduce_fusion.perm, f32[32,16,4096]{2,1,0:T(8,128)} %state_ref.4, f32[32,4096]{1,0:T(8,128)S(1)} %get-tuple-element.18.dt_ref, f32[32,4096]{1,0:T(8,128)S(1)} %get-tuple-element.19.signal_ref, ...), custom_call_target="tpu_custom_call" | custom-call | flops 8388608 | bytes 8388608 | tf_op jit(solution)/shard_map/ssm_early/pallas_call | solution.py:350
  102.4 0.8 copy-done.9
  103.3 0.7 gather_fusion.2
  103.9 0.7 bitcast_select_fusion
  104.7 0.0 all-to-all-done.1
  104.7 1.0 copy-done.7
  105.7 1.0 copy-done.10
  106.8 0.8 copy-done.14
  107.5 0.6 copy-done.20
  108.1 0.7 copy-done.22
  108.8 12.0 %ssm_late.1 = (f32[32,16,4096]{2,1,0:T(8,128)}, bf16[32,4096]{1,0:T(8,128)(2,1)}) custom-call(s32[32]{0:T(128)S(1)} %copy-done.22, s32[32]{0:T(128)S(1)} %copy-done.20, f32[32,16,4096]{2,1,0:T(8,128)} %state_ref.4, bf16[16,16,4096]{2,1,0:T(8,128)(2,1)S(1)} %bitcast.21, f32[32,4096]{1,0:T(8,128)S(1)} %get-tuple-element.18.dt_ref, ...), custom_call_target="tpu_custom_call", output_to_operand_aliasing={{0}: (11, {})} | custom-call | flops 8388608 | bytes 10485760 | tf_op jit(solution)/shard_map/ssm_late/pallas_call | solution.py:379
  (50 shorter events, 0.2 us)
Async XLA Ops:
  0.6 4.2 %copy-start = (bf16[16,3,4096]{2,0,1:T(8,128)(2,1)S(1)}, bf16[16,3,4096]{2,0,1:T(8,128)(2,1)}, u32[]{:S(2)}) copy-start(bf16[16,3,4096]{2,0,1:T(8,128)(2,1)} %param.29) | copy-start | bytes 1179652
  2.0 74.5 %copy-start.19 = (s32[32]{0:T(128)}, s32[32]{0:T(128)S(1)}, u32[]{:S(2)}) copy-start(s32[32]{0:T(128)S(1)} %get-tuple-element.39.source) | copy-start | bytes 388
  4.5 10.9 %copy-start.30 = (s32[1,8,2,32]{3,2,1,0:T(2,128)S(1)}, s32[1,8,2,32]{3,2,1,0:T(2,128)}, u32[]{:S(2)}) copy-start(s32[1,8,2,32]{3,2,1,0:T(2,128)} %param.51) | copy-start | bytes 6148
  4.5 11.0 %copy-start.32 = (s32[1,8,2]{1,2,0:T(2,128)S(1)}, s32[1,8,2]{1,2,0:T(2,128)}, u32[]{:S(2)}) copy-start(s32[1,8,2]{1,2,0:T(2,128)} %param.50) | copy-start | bytes 196
  8.2 21.7 %all-to-all-start = ((bf16[8,2,4,4096]{3,2,1,0:T(4,128)(2,1)}), bf16[8,2,4,4096]{3,2,1,0:T(4,128)(2,1)S(1)}, u32[]{:S(2)}, u32[]{:S(2)}) async-start(bf16[8,2,4,4096]{3,2,1,0:T(4,128)(2,1)} %pad_maximum_fusion), calls=%async_computation | async-start | bytes 1048576 | tf_op jit(solution)/shard_map/all_to_all | solution.py:464
  29.9 19.0 %copy-start.4 = (bf16[8,2,4,4096]{3,2,1,0:T(4,128)(2,1)}, bf16[8,2,4,4096]{3,2,1,0:T(4,128)(2,1)S(1)}, u32[]{:S(2)}) copy-start(bf16[8,2,4,4096]{3,2,1,0:T(4,128)(2,1)S(1)} %all-to-all-done) | copy-start | bytes 1572868
  30.4 22.1 %copy-start.29 = (bf16[32,512]{1,0:T(8,128)(2,1)S(1)}, bf16[32,512]{1,0:T(8,128)(2,1)}, u32[]{:S(2)}) copy-start(bf16[32,512]{1,0:T(8,128)(2,1)} %param.43) | copy-start | bytes 98308
  30.4 22.1 %copy-start.27 = (bf16[32,2048]{1,0:T(8,128)(2,1)S(1)}, bf16[32,2048]{1,0:T(8,128)(2,1)}, u32[]{:S(2)}) copy-start(bf16[32,2048]{1,0:T(8,128)(2,1)} %param.42) | copy-start | bytes 393220
  30.5 2.2 %copy-start.2 = (bf16[256,16,512]{2,1,0:T(8,128)(2,1)S(1)}, bf16[256,16,512]{2,1,0:T(8,128)(2,1)}, u32[]{:S(2)}) copy-start(bf16[256,16,512]{2,1,0:T(8,128)(2,1)} %pool_ref.3) | copy-start | bytes 12582916
  48.9 55.7 %all-to-all-start.1 = ((bf16[8,2,16,4096]{3,2,1,0:T(8,128)(2,1)}), bf16[8,2,16,4096]{3,2,1,0:T(8,128)(2,1)S(1)}, u32[]{:S(2)}, u32[]{:S(2)}) async-start(bf16[8,2,16,4096]{3,2,1,0:T(8,128)(2,1)} %bitcast.2), calls=%async_computation.1 | async-start | bytes 4194304 | tf_op jit(solution)/shard_map/all_to_all | solution.py:464
  54.4 7.6 %copy-start.24 = (s32[32]{0:T(128)S(1)}, s32[32]{0:T(128)}, u32[]{:S(2)}) copy-start(s32[32]{0:T(128)} %lens.1) | copy-start | bytes 388
  62.0 13.6 %copy-start.31 = (s32[32]{0:T(128)S(1)}, s32[32]{0:T(128)}, u32[]{:S(2)}) copy-start(s32[32]{0:T(128)} %param.47) | copy-start | bytes 388
  62.0 14.6 %copy-start.5 = (bf16[8,2,4,4096]{3,2,1,0:T(4,128)(2,1)S(1)}, bf16[8,2,4,4096]{3,2,1,0:T(4,128)(2,1)}, u32[]{:S(2)}) copy-start(bf16[8,2,4,4096]{3,2,1,0:T(4,128)(2,1)} %copy-done.4) | copy-start | bytes 1572868
  62.0 14.6 %copy-start.12 = (bf16[32,4096]{1,0:T(8,128)(2,1)S(1)}, bf16[32,4096]{1,0:T(8,128)(2,1)}, u32[]{:S(2)}) copy-start(bf16[32,4096]{1,0:T(8,128)(2,1)} %x_ref.1) | copy-start | bytes 786436
  62.0 14.6 %copy-start.15 = (bf16[4,4096]{1,0:T(4,128)(2,1)S(1)}, bf16[4,4096]{1,0:T(4,128)(2,1)}, u32[]{:S(2)}) copy-start(bf16[4,4096]{1,0:T(4,128)(2,1)} %weight_ref.1) | copy-start | bytes 98308
  62.0 14.6 %copy-start.16 = (f32[4096]{0:T(1024)S(1)}, f32[4096]{0:T(1024)}, u32[]{:S(2)}) copy-start(f32[4096]{0:T(1024)} %param.33) | copy-start | bytes 49156
  76.5 14.5 %copy-start.21 = (s32[32]{0:T(128)}, s32[32]{0:T(128)S(1)}, u32[]{:S(2)}) copy-start(s32[32]{0:T(128)S(1)} %select_reduce_fusion.perm) | copy-start | bytes 388
  76.6 8.1 %copy-start.3 = (bf16[512,4096]{1,0:T(8,128)(2,1)S(1)}, bf16[512,4096]{1,0:T(8,128)(2,1)}, u32[]{:S(2)}) copy-start(bf16[512,4096]{1,0:T(8,128)(2,1)} %dt_proj_ref.1) | copy-start | bytes 12582916
  76.6 8.1 %copy-start.17 = (f32[4096]{0:T(1024)S(1)}, f32[4096]{0:T(1024)}, u32[]{:S(2)}) copy-start(f32[4096]{0:T(1024)} %param.39) | copy-start | bytes 49156
  76.6 8.1 %copy-start.23 = (f32[512]{0:T(512)S(1)}, f32[512]{0:T(512)}, u32[]{:S(2)}) copy-start(f32[512]{0:T(512)} %param.35) | copy-start | bytes 6148
  76.6 8.1 %copy-start.25 = (f32[16]{0:T(128)S(1)}, f32[16]{0:T(128)}, u32[]{:S(2)}) copy-start(f32[16]{0:T(128)} %param.36) | copy-start | bytes 196
  76.6 8.1 %copy-start.26 = (f32[16]{0:T(128)S(1)}, f32[16]{0:T(128)}, u32[]{:S(2)}) copy-start(f32[16]{0:T(128)} %param.37) | copy-start | bytes 196
  83.2 7.9 %copy-start.6 = (f32[32,4096]{1,0:T(8,128)}, f32[32,4096]{1,0:T(8,128)S(1)}, u32[]{:S(2)}) copy-start(f32[32,4096]{1,0:T(8,128)S(1)} %get-tuple-element.19.signal_ref) | copy-start | bytes 1572868
  83.2 7.9 %copy-start.8 = (f32[16,4096]{1,0:T(8,128)S(1)}, f32[16,4096]{1,0:T(8,128)}, u32[]{:S(2)}) copy-start(f32[16,4096]{1,0:T(8,128)} %decay_ref.3) | copy-start | bytes 786436
  91.1 11.4 %copy-start.13 = (f32[2,32,16]{2,1,0:T(8,128)}, f32[2,32,16]{2,1,0:T(8,128)S(1)}, u32[]{:S(2)}) copy-start(f32[2,32,16]{2,1,0:T(8,128)S(1)} %get-tuple-element.20.bc_ref) | copy-start | bytes 12292
  91.1 12.1 %copy-start.28 = (bf16[8,2,2048]{2,1,0:T(2,128)(2,1)S(1)}, bf16[8,2,2048]{2,1,0:T(2,128)(2,1)}, u32[]{:S(2)}) copy-start(bf16[8,2,2048]{2,1,0:T(2,128)(2,1)} %all_to_all.15) | copy-start | bytes 196612
  91.1 13.5 %copy-start.11 = (bf16[32,4096]{1,0:T(8,128)(2,1)S(1)}, bf16[32,4096]{1,0:T(8,128)(2,1)}, u32[]{:S(2)}) copy-start(bf16[32,4096]{1,0:T(8,128)(2,1)} %z_ref.1) | copy-start | bytes 786436
  91.1 13.5 %copy-start.18 = (f32[4096]{0:T(1024)S(1)}, f32[4096]{0:T(1024)}, u32[]{:S(2)}) copy-start(f32[4096]{0:T(1024)} %param.41) | copy-start | bytes 49156
  102.4 0.8 copy-start.9
  104.7 1.0 copy-start.7
  105.7 1.0 copy-start.10
  106.7 0.8 copy-start.14
  107.5 0.6 copy-start.20
  108.1 0.7 copy-start.22
  108.8 12.0 %copy-start.1 = (bf16[16,3,4096]{2,0,1:T(8,128)(2,1)S(1)}, bf16[16,3,4096]{2,0,1:T(8,128)(2,1)}, u32[]{:S(2)}) copy-start(bf16[16,3,4096]{2,0,1:T(8,128)(2,1)} %param.29) | copy-start | bytes 1179652

commit v2 on v1

--- a/solution.py
+++ b/solution.py
@@ -10,6 +10,7 @@
 
 HD = 128
 MESH = pl.DeviceIdType.MESH
+BATCH = 4
 VMEM_LIMIT = 48 * 1024 * 1024
 
 
@@ -101,7 +102,7 @@
 def attend_resident(q, kv, nkv, lens):
     rows, heads, width = q.shape
     tokens, kv_width = kv.shape[1:]
-    batch = 4
+    batch = BATCH
     return pl.pallas_call(
         resident_kernel,
         grid_spec=pltpu.PrefetchScalarGridSpec(
@@ -127,7 +128,7 @@
 
 def attend_paged(q, pool, nkv, lens, pages, tokens):
     entries, heads, width = q.shape
-    batch = 4
+    batch = BATCH
     return pl.pallas_call(
         paged_kernel,
         grid_spec=pltpu.PrefetchScalarGridSpec(
@@ -152,20 +153,26 @@
     )(lens, pages, q, pool, nkv)
 
 
-def pack_kernel(slots, pool_ref, out_ref):
-    out_ref[...] = pool_ref[...].astype(jnp.bfloat16)
+def pack_kernel(slots, *refs):
+    out_ref = refs[-1]
+    for k, ref in enumerate(refs[:-1]):
+        out_ref[k] = ref[0].astype(jnp.bfloat16)
 
 
 def pack_states(pool, slots):
     entries = slots.shape[0]
     block = (1,) + pool.shape[1:]
+
+    def spec(k):
+        return pl.BlockSpec(block, lambda i, slots: (slots[i * BATCH + k], 0, 0))
+
     return pl.pallas_call(
         pack_kernel,
         grid_spec=pltpu.PrefetchScalarGridSpec(
             num_scalar_prefetch=1,
-            grid=(entries,),
-            in_specs=[pl.BlockSpec(block, lambda i, slots: (slots[i], 0, 0))],
-            out_specs=pl.BlockSpec(block, lambda i, slots: (i, 0, 0)),
+            grid=(entries // BATCH,),
+            in_specs=[spec(k) for k in range(BATCH)],
+            out_specs=pl.BlockSpec((BATCH,) + pool.shape[1:], lambda i, slots: (i, 0, 0)),
         ),
         out_shape=jax.ShapeDtypeStruct((entries,) + pool.shape[1:], jnp.bfloat16),
         compiler_params=params(),
@@ -173,79 +180,139 @@
             flops=0, bytes_accessed=6 * entries * pool[0].size, transcendentals=0
         ),
         name="pack_states",
-    )(slots, pool)
-
-
-def conv_kernel(source, x_ref, state_ref, got_ref, weight_ref, bias_ref, proj_ref,
-                mixed_ref, conv_ref, part_ref, sum_ref):
-    rows, taps = state_ref.shape[:2]
-    weight = weight_ref[...].astype(jnp.float32)
-    for r in range(rows):
-        entry = source[r]
-        prev = jnp.where(
-            entry >= 0,
-            got_ref[jnp.maximum(entry, 0)].astype(jnp.float32)[:taps],
-            state_ref[r].astype(jnp.float32),
+    )(slots, *([pool] * BATCH))
+
+
+def entry_match(owner_ref, pos_ref, entries, cap):
+    owner = owner_ref[...]
+    source = jnp.where(owner >= 0, owner * cap + pos_ref[...], -1)
+    shape = (entries, owner.shape[1])
+    hit = lax.broadcasted_iota(jnp.int32, shape, 0) == jnp.broadcast_to(source, shape)
+    return jnp.where(hit, 1.0, 0.0).astype(jnp.bfloat16)
+
+
+def pick(match, rows, contract):
+    return lax.dot_general(
+        match, rows, (((contract,), (0,)), ((), ())), preferred_element_type=jnp.float32
+    )
+
+
+def ask_kernel(cap, owner_ref, pos_ref, slot_ref, pool_ref, query_ref, new_ref, out_ref):
+    taps, slots, channels = pool_ref.shape
+    entries = out_ref.shape[0]
+    shape = (slots, entries)
+    hit = lax.broadcasted_iota(jnp.int32, shape, 0) == jnp.broadcast_to(slot_ref[...], shape)
+    chosen = jnp.where(hit, 1.0, 0.0).astype(jnp.bfloat16)
+    for j in range(taps):
+        out_ref[:, j * channels : (j + 1) * channels] = pick(chosen, pool_ref[j], 0).astype(
+            jnp.bfloat16
         )
-        new = x_ref[r : r + 1, :].astype(jnp.float32)
-        conv_ref[r] = jnp.concatenate([prev[1:], new], axis=0).astype(jnp.bfloat16)
-        sum_ref[r : r + 1, :] = (
-            jnp.sum(prev * weight[:taps], axis=0, keepdims=True) + new * weight[taps:]
-        )
-    total = sum_ref[...] + bias_ref[...]
+    match = entry_match(owner_ref, pos_ref, entries, cap)
+    at = taps * channels
+    for ref in (query_ref, new_ref):
+        out_ref[:, at : at + ref.shape[1]] = pick(match, ref[...], 1).astype(jnp.bfloat16)
+        at += ref.shape[1]
+
+
+def ask(cap, owner, pos, slots, pool, query, new_kv):
+    entries = slots.shape[1]
+    operands = (owner, pos, slots, pool, query, new_kv)
+    width = pool.shape[0] * pool.shape[2] + query.shape[1] + new_kv.shape[1]
+    return pl.pallas_call(
+        functools.partial(ask_kernel, cap),
+        grid=(1,),
+        in_specs=[whole(a.shape) for a in operands],
+        out_specs=whole((entries, width)),
+        out_shape=jax.ShapeDtypeStruct((entries, width), jnp.bfloat16),
+        compiler_params=params(),
+        cost_estimate=pl.CostEstimate(
+            flops=2 * entries * pool.size, bytes_accessed=4 * pool.size, transcendentals=0
+        ),
+        name="ask",
+    )(*operands)
+
+
+def conv_kernel(cap, owner_ref, pos_ref, x_ref, state_ref, got_ref, weight_ref, bias_ref,
+                proj_ref, mixed_ref, conv_ref, part_ref):
+    taps, rows, channels = state_ref.shape
+    entries = got_ref.shape[0]
+    match = entry_match(owner_ref, pos_ref, entries, cap)
+    resumed = pick(match, jnp.ones((entries, 128), jnp.bfloat16), 0)[:, :1] > 0.5
+    new = x_ref[...]
+    total = new.astype(jnp.float32) * weight_ref[taps : taps + 1, :].astype(jnp.float32)
+    for j in range(taps):
+        theirs = pick(match, got_ref[:, j * channels : (j + 1) * channels], 0)
+        prev = jnp.where(resumed, theirs, state_ref[j].astype(jnp.float32))
+        if j > 0:
+            conv_ref[j - 1] = prev.astype(jnp.bfloat16)
+        total = total + prev * weight_ref[j : j + 1, :].astype(jnp.float32)
+    conv_ref[taps - 1] = new
+    total = total + bias_ref[...]
     mixed = (total / (1.0 + jnp.exp(-total))).astype(jnp.bfloat16)
     mixed_ref[...] = mixed.astype(jnp.float32)
-    part_ref[...] = jnp.dot(mixed, proj_ref[...], preferred_element_type=jnp.float32)
-
-
-def convolve(source, x_in, state, got, weight, bias, x_proj):
+    part_ref[...] = lax.dot_general(
+        mixed, proj_ref[...], (((1,), (1,)), ((), ())), preferred_element_type=jnp.float32
+    )
+
+
+def convolve(cap, owner, pos, x_in, state, got, weight, bias, proj):
     rows, channels = x_in.shape
     outs = (
         jax.ShapeDtypeStruct((rows, channels), jnp.float32),
         jax.ShapeDtypeStruct(state.shape, jnp.bfloat16),
-        jax.ShapeDtypeStruct((rows, x_proj.shape[1]), jnp.float32),
-    )
-    operands = (x_in, state, got, weight, bias, x_proj)
-    return pl.pallas_call(
-        conv_kernel,
-        grid_spec=pltpu.PrefetchScalarGridSpec(
-            num_scalar_prefetch=1,
-            grid=(1,),
-            in_specs=[whole(a.shape) for a in operands],
-            out_specs=[whole(o.shape) for o in outs],
-            scratch_shapes=[pltpu.VMEM((rows, channels), jnp.float32)],
-        ),
+        jax.ShapeDtypeStruct((rows, proj.shape[0]), jnp.float32),
+    )
+    operands = (owner, pos, x_in, state, got, weight, bias, proj)
+    return pl.pallas_call(
+        functools.partial(conv_kernel, cap),
+        grid=(1,),
+        in_specs=[whole(a.shape) for a in operands],
+        out_specs=[whole(o.shape) for o in outs],
         out_shape=outs,
         compiler_params=params(),
         cost_estimate=pl.CostEstimate(
-            flops=2 * rows * x_proj.size, bytes_accessed=2 * x_proj.size + 8 * x_in.size * 2,
+            flops=2 * rows * proj.size, bytes_accessed=2 * proj.size + 16 * x_in.size,
             transcendentals=x_in.size,
         ),
         name="conv_proj",
-    )(source, *operands)
-
-
-def step_kernel(count, part_ref, dt_proj_ref, bias_ref, dt_gain_ref, b_gain_ref, c_gain_ref,
-                dt_ref, bc_ref, got_ref, send_sem, recv_sem):
+    )(*operands)
+
+
+def step_kernel(count, peers, part_ref, attn_ref, dt_proj_ref, bias_ref, dt_gain_ref, b_gain_ref,
+                c_gain_ref, dt_ref, bc_ref, back_ref, got_ref, home_ref, send_sem, recv_sem,
+                home_send, home_recv):
     me = lax.axis_index("tp")
+    group = lax.axis_index("rep")
     barrier = pltpu.get_barrier_semaphore()
-    for k in range(1, count):
-        pl.semaphore_signal(
-            barrier, inc=1, device_id={"tp": lax.rem(me + k, count)}, device_id_type=MESH
-        )
-    pl.semaphore_wait(barrier, count - 1)
+    partners = [{"tp": lax.rem(me + k, count)} for k in range(1, count)]
+    homes = [lax.rem(group + k, peers) for k in range(1, peers)]
+    for partner in partners + [{"rep": home} for home in homes]:
+        pl.semaphore_signal(barrier, inc=1, device_id=partner, device_id_type=MESH)
+    pl.semaphore_wait(barrier, count + peers - 2)
     copies = []
-    for k in range(1, count):
+    for k, partner in enumerate(partners):
         copy = pltpu.make_async_remote_copy(
             src_ref=part_ref,
-            dst_ref=got_ref.at[k - 1],
-            send_sem=send_sem.at[k - 1],
-            recv_sem=recv_sem.at[k - 1],
-            device_id={"tp": lax.rem(me + k, count)},
+            dst_ref=got_ref.at[k],
+            send_sem=send_sem.at[k],
+            recv_sem=recv_sem.at[k],
+            device_id=partner,
             device_id_type=MESH,
         )
         copy.start()
         copies.append(copy)
+    returns = []
+    for k, home in enumerate(homes):
+        copy = pltpu.make_async_remote_copy(
+            src_ref=attn_ref.at[home],
+            dst_ref=home_ref.at[k],
+            send_sem=home_send.at[k],
+            recv_sem=home_recv.at[k],
+            device_id={"rep": home},
+            device_id_type=MESH,
+        )
+        copy.start()
+        returns.append(copy)
     proj = part_ref[...]
     for k, copy in enumerate(copies):
         copy.wait_recv()
@@ -262,26 +329,35 @@
     dt_ref[...] = jnp.maximum(raw, 0.0) + jnp.log1p(jnp.exp(-jnp.abs(raw)))
     bc_ref[0] = rms_scaled(proj[:, rank : rank + states], b_gain_ref[...]).astype(jnp.float32)
     bc_ref[1] = rms_scaled(proj[:, rank + states :], c_gain_ref[...]).astype(jnp.float32)
-    for copy in copies:
+    back_ref[group] = attn_ref[group]
+    for k, copy in enumerate(returns):
+        copy.wait_recv()
+        back_ref[lax.rem(group + peers - 1 - k, peers)] = home_ref[k]
+    for copy in copies + returns:
         copy.wait_send()
 
 
-def step_sizes(count, part, dt_proj, dt_bias, dt_gain, b_gain, c_gain):
+def step_sizes(count, part, attn, dt_proj, dt_bias, dt_gain, b_gain, c_gain):
     rows = part.shape[0]
+    peers = attn.shape[0]
     channels = dt_proj.shape[1]
     vmem = pl.BlockSpec(memory_space=pltpu.VMEM)
     return pl.pallas_call(
-        functools.partial(step_kernel, count),
+        functools.partial(step_kernel, count, peers),
         out_shape=(
             jax.ShapeDtypeStruct((rows, channels), jnp.float32),
             jax.ShapeDtypeStruct((2, rows, b_gain.shape[1]), jnp.float32),
-        ),
-        in_specs=[vmem] * 6,
-        out_specs=(vmem, vmem),
+            jax.ShapeDtypeStruct(attn.shape, jnp.bfloat16),
+        ),
+        in_specs=[vmem] * 7,
+        out_specs=(vmem, vmem, vmem),
         scratch_shapes=[
             pltpu.VMEM((count - 1,) + part.shape, jnp.float32),
+            pltpu.VMEM((peers - 1,) + attn.shape[1:], jnp.bfloat16),
             pltpu.SemaphoreType.DMA((count - 1,)),
             pltpu.SemaphoreType.DMA((count - 1,)),
+            pltpu.SemaphoreType.DMA((peers - 1,)),
+            pltpu.SemaphoreType.DMA((peers - 1,)),
         ],
         compiler_params=params(collective_id=0, has_side_effects=True),
         cost_estimate=pl.CostEstimate(
@@ -289,7 +365,7 @@
             transcendentals=2 * rows * channels,
         ),
         name="tp_sum_step",
-    )(part, dt_proj, dt_bias, dt_gain, b_gain, c_gain)
+    )(part, attn, dt_proj, dt_bias, dt_gain, b_gain, c_gain)
 
 
 def update_row(row, prev, dt_ref, signal_ref, bc_ref, decay_ref):
@@ -309,32 +385,76 @@
     return new, jnp.sum(column(1) * new, axis=0, keepdims=True)
 
 
-def early_kernel(perm, state_ref, dt_ref, signal_ref, bc_ref, decay_ref, new_ref, y_ref, *, first):
+def write_rows(perm, first, news, new_ref, buf_ref, sem):
+    step, steps = pl.program_id(0), pl.num_programs(0)
+
+    def copies(at):
+        slot = lax.rem(at, 2)
+        return [
+            pltpu.make_async_copy(
+                buf_ref.at[slot, k], new_ref.at[perm[first + at * BATCH + k]], sem.at[slot, k]
+            )
+            for k in range(BATCH)
+        ]
+
+    @pl.when(step >= 2)
+    def _():
+        for copy in copies(step - 2):
+            copy.wait()
+
+    here = copies(step)
+    slot = lax.rem(step, 2)
+    for k in range(BATCH):
+        buf_ref[slot, k] = news(k)
+        here[k].start()
+
+    @pl.when(step == steps - 1)
+    def _():
+        @pl.when(step >= 1)
+        def _():
+            for copy in copies(step - 1):
+                copy.wait()
+
+        for copy in here:
+            copy.wait()
+
+
+def early_kernel(first, perm, *refs):
+    states = refs[:BATCH]
+    dt_ref, signal_ref, bc_ref, decay_ref, new_ref, y_ref, buf_ref, sem = refs[BATCH:]
     step = pl.program_id(0)
 
     @pl.when(step == 0)
     def _():
         y_ref[...] = jnp.zeros_like(y_ref)
 
-    row = perm[first + step]
-    new, y = update_row(row, state_ref[0], dt_ref, signal_ref, bc_ref, decay_ref)
-    new_ref[0] = new
-    y_ref[pl.ds(row, 1), :] = y
-
-
-def late_kernel(perm, source, state_ref, got_ref, dt_ref, signal_ref, bc_ref, decay_ref, early_y,
-                skip_ref, z_ref, kept_ref, new_ref, out_ref, y_ref):
+    def news(k):
+        row = perm[first + step * BATCH + k]
+        new, y = update_row(row, states[k][0], dt_ref, signal_ref, bc_ref, decay_ref)
+        y_ref[pl.ds(row, 1), :] = y
+        return new
+
+    write_rows(perm, first, news, new_ref, buf_ref, sem)
+
+
+def late_kernel(perm, source, *refs):
+    states, gots = refs[:BATCH], refs[BATCH : 2 * BATCH]
+    (dt_ref, signal_ref, bc_ref, decay_ref, early_y, skip_ref, z_ref, kept_ref, new_ref, out_ref,
+     y_ref, buf_ref, sem) = refs[2 * BATCH :]
     step = pl.program_id(0)
 
     @pl.when(step == 0)
     def _():
         y_ref[...] = early_y[...]
 
-    row = perm[step]
-    prev = jnp.where(source[row] >= 0, got_ref[0].astype(jnp.float32), state_ref[0])
-    new, y = update_row(row, prev, dt_ref, signal_ref, bc_ref, decay_ref)
-    new_ref[0] = new
-    y_ref[pl.ds(row, 1), :] = y
+    def news(k):
+        row = perm[step * BATCH + k]
+        prev = jnp.where(source[row] >= 0, gots[k][0].astype(jnp.float32), states[k][0])
+        new, y = update_row(row, prev, dt_ref, signal_ref, bc_ref, decay_ref)
+        y_ref[pl.ds(row, 1), :] = y
+        return new
+
+    write_rows(perm, 0, news, new_ref, buf_ref, sem)
 
     @pl.when(step == pl.num_programs(0) - 1)
     def _():
@@ -347,16 +467,20 @@
     rows = state.shape[0]
     block = (1,) + state.shape[1:]
     shared = (dt, signal, bc, decay)
-    return pl.pallas_call(
-        functools.partial(early_kernel, first=late),
+
+    def spec(k):
+        return pl.BlockSpec(block, lambda i, perm: (perm[late + i * BATCH + k], 0, 0))
+
+    return pl.pallas_call(
+        functools.partial(early_kernel, late),
         grid_spec=pltpu.PrefetchScalarGridSpec(
             num_scalar_prefetch=1,
-            grid=(rows - late,),
-            in_specs=[pl.BlockSpec(block, lambda i, perm: (perm[late + i], 0, 0))]
-            + [whole(a.shape) for a in shared],
-            out_specs=[
-                pl.BlockSpec(block, lambda i, perm: (perm[late + i], 0, 0)),
-                whole(dt.shape),
+            grid=((rows - late) // BATCH,),
+            in_specs=[spec(k) for k in range(BATCH)] + [whole(a.shape) for a in shared],
+            out_specs=[pl.BlockSpec(memory_space=pl.ANY), whole(dt.shape)],
+            scratch_shapes=[
+                pltpu.VMEM((2, BATCH) + state.shape[1:], jnp.float32),
+                pltpu.SemaphoreType.DMA((2, BATCH)),
             ],
         ),
         out_shape=(
@@ -370,36 +494,43 @@
             transcendentals=(rows - late) * state[0].size,
         ),
         name="ssm_early",
-    )(perm, state, *shared)
+    )(perm, *([state] * BATCH), *shared)
 
 
 def update_late(perm, source, state, got, dt, signal, bc, decay, early_y, skip, z, kept, late):
     block = (1,) + state.shape[1:]
     shared = (dt, signal, bc, decay, early_y, skip, z)
+
+    def state_spec(k):
+        return pl.BlockSpec(block, lambda i, perm, source: (perm[i * BATCH + k], 0, 0))
+
+    def got_spec(k):
+        return pl.BlockSpec(
+            block,
+            lambda i, perm, source: (jnp.maximum(source[perm[i * BATCH + k]], 0), 0, 0),
+        )
+
     return pl.pallas_call(
         late_kernel,
         grid_spec=pltpu.PrefetchScalarGridSpec(
             num_scalar_prefetch=2,
-            grid=(late,),
-            in_specs=[
-                pl.BlockSpec(block, lambda i, perm, source: (perm[i], 0, 0)),
-                pl.BlockSpec(
-                    block, lambda i, perm, source: (jnp.maximum(source[perm[i]], 0), 0, 0)
-                ),
-            ]
+            grid=(late // BATCH,),
+            in_specs=[state_spec(k) for k in range(BATCH)]
+            + [got_spec(k) for k in range(BATCH)]
             + [whole(a.shape) for a in shared]
             + [pl.BlockSpec(memory_space=pl.ANY)],
-            out_specs=[
-                pl.BlockSpec(block, lambda i, perm, source: (perm[i], 0, 0)),
-                whole(dt.shape),
+            out_specs=[pl.BlockSpec(memory_space=pl.ANY), whole(dt.shape)],
+            scratch_shapes=[
+                pltpu.VMEM(dt.shape, jnp.float32),
+                pltpu.VMEM((2, BATCH) + state.shape[1:], jnp.float32),
+                pltpu.SemaphoreType.DMA((2, BATCH)),
             ],
-            scratch_shapes=[pltpu.VMEM(dt.shape, jnp.float32)],
         ),
         out_shape=(
             jax.ShapeDtypeStruct(state.shape, jnp.float32),
             jax.ShapeDtypeStruct(dt.shape, jnp.bfloat16),
         ),
-        input_output_aliases={4 + len(shared): 0},
+        input_output_aliases={2 + 2 * BATCH + len(shared): 0},
         compiler_params=params(),
         cost_estimate=pl.CostEstimate(
             flops=8 * late * state[0].size,
@@ -407,7 +538,7 @@
             transcendentals=late * state[0].size,
         ),
         name="ssm_late",
-    )(perm, source, state, got, *shared, kept)
+    )(perm, source, *([state] * BATCH), *([got] * BATCH), *shared, kept)
 
 
 def shards(
@@ -449,9 +580,6 @@
     resumed = row_owner >= 0
     source = jnp.where(resumed, row_owner * slot_cap + row_pos, -1).astype(jnp.int32)
     row_ids = jnp.arange(row_count, dtype=jnp.int32)
-    entry_ids = jnp.arange(entry_count, dtype=jnp.int32)
-    match = source[None, :] == entry_ids[:, None]
-    entry_row = jnp.sum(jnp.where(match, row_ids[None, :], 0), axis=1)
     before = row_ids[None, :] < row_ids[:, None]
     earlier = jnp.sum((before & (resumed[None, :] == resumed[:, None])).astype(jnp.int32), axis=1)
     place = jnp.where(resumed, earlier, earlier + jnp.sum(resumed.astype(jnp.int32)))
@@ -464,11 +592,13 @@
         out = lax.all_to_all(split, "rep", split_axis=0, concat_axis=0, tiled=True)
         return out.reshape(block.shape)
 
-    asked = jnp.take(jnp.concatenate([query, new_kv], axis=1), entry_row, axis=0, mode="clip")
-    asked = jnp.pad(asked, ((0, 0), (0, channels - asked.shape[1])))
-    taps_out = jnp.take(conv_pool, slot_list, axis=0, mode="clip")
-    first = exchange(jnp.concatenate([taps_out, asked[:, None, :]], axis=1))
-
+    owner_line, pos_line = row_owner[None, :], row_pos[None, :]
+    first = exchange(
+        ask(
+            slot_cap, owner_line, pos_line, slot_list[None, :], jnp.swapaxes(conv_pool, 0, 1),
+            query, new_kv,
+        )
+    )
     states = pack_states(ssm_pool, slot_list)
     first, states = lax.optimization_barrier((first, states))
     states_in = exchange(states)
@@ -478,22 +608,24 @@
     attn_here = attend_resident(query_rows, kv_cache, new_rows, ctx_len).reshape(query.shape)
 
     mixed, new_conv, part = convolve(
-        source, x_in, conv_state, first, conv_weight, conv_bias[None, :], x_proj
-    )
-    dt_step, bc = step_sizes(
-        tp_count, part, dt_proj, dt_bias[None, :], dt_gain[None, :], b_gain[None, :],
-        c_gain[None, :],
-    )
+        slot_cap, owner_line, pos_line, x_in, jnp.swapaxes(conv_state, 0, 1), first, conv_weight,
+        conv_bias[None, :], x_proj.T,
+    )
+    new_conv = jnp.swapaxes(new_conv, 0, 1)
 
     query_width = query.shape[1]
-    asked_in = first[:, taps, :]
-    query_in = asked_in[:, :query_width].reshape(entry_count, head_count, HD)
-    new_in = asked_in[:, query_width : query_width + new_kv.shape[1]].reshape(entry_count, -1, HD)
+    asked = first[:, taps * channels :]
+    query_in = asked[:, :query_width].reshape(entry_count, head_count, HD)
+    new_in = asked[:, query_width:].reshape(entry_count, -1, HD)
     attn_there = attend_paged(
         query_in, kv_pool, new_in, swap_lens[0].reshape(-1), swap_pages[0].reshape(-1),
         kv_cache.shape[1],
-    ).reshape(entry_count, query_width)
-    attn_back = exchange(attn_there)
+    )
+    dt_step, bc, attn_back = step_sizes(
+        tp_count, part, attn_there.reshape(peer_count, slot_cap, head_count, HD), dt_proj,
+        dt_bias[None, :], dt_gain[None, :], b_gain[None, :], c_gain[None, :],
+    )
+    attn_back = attn_back.reshape(entry_count, query_width)
     picked = jnp.take(attn_back, jnp.maximum(source, 0), axis=0, mode="clip")
     attn_out = jnp.where(resumed[:, None], picked, attn_here)
 

time: 123 us -> 103 us (0.84)
  blocking collectives: 10.4 us -> 0 us
  Pallas kernels: 65.8 us -> 60.5 us
  local copies, waits for them, and re-layouts: 23.2 us -> 18.2 us
  waiting for transfers between devices: 3.87 us -> 8.47 us
  other arithmetic: 5.46 us -> 2.92 us
    all_to_all x1 -> x0, blocking collectives: 10.4 us -> none  [exchange(): out = lax.all_to_all(split, 'rep', split_axis=0, concat_axis=0, tiled=True)]
    pallas_call x1, Pallas kernels: 10.4 us -> 3.5 us  [pack_states(): pl.pallas_call(pack_kernel, grid_spec=pltpu.PrefetchScalarGridSpec(num_sc...]
    pallas_call x3 -> x4, Pallas kernels: 24.2 us -> 30.6 us  [the longest x1 20.1 us: step_sizes(): pl.pallas_call(functools.partial(step_kernel, count, peers), out_shape=(j...]
    pallas_call x1, Pallas kernels: 12 us -> 7.14 us  [update_late(): pl.pallas_call(late_kernel, grid_spec=pltpu.PrefetchScalarGridSpec(num_sc...]
    all_to_all x2, waiting for transfers between devices: 3.87 us -> 8.47 us  [exchange(): out = lax.all_to_all(split, 'rep', split_axis=0, concat_axis=0, tiled=True)]
    unnamed x75 -> x74, local copies, waits for them, and re-layouts: 19.1 us -> 15.3 us
    gather x2 -> x0, local copies, waits for them, and re-layouts: 2.29 us -> none  [the longest x1 1.69 us: shards(): taps_out = jnp.take(conv_pool, slot_list, axis=0, mode='clip')]
    concatenate x2 -> x0, other arithmetic: 2.28 us -> none  [the longest x1 1.34 us: shards(): first = exchange(jnp.concatenate([taps_out, asked[:, None, :]], axis=1))]
  transfers between devices with their start and end apart: 2 -> 2, of which waited for: 1 -> 1; matrix products, arithmetic and copies ran while one was open for 11% -> 5% of each run, Pallas kernels for 40% -> 52%
where the time goes in v2:
time: 103 us; the launch traced here: 102 us
  Pallas kernels  60.5 us (59%)
  local copies, waits for them, and re-layouts  18.2 us (18%)
  starting transfers between devices  10.9 us (11%)
  waiting for transfers between devices  8.47 us (8%)
  other arithmetic  2.92 us (3%)
    pallas_call x1, Pallas kernels, step_sizes(): pl.pallas_call(functools.partial(step_kernel, count, peers), out_shape=(j...  20.1 us
    unnamed x74, local copies, waits for them, and re-layouts  15.3 us
    pallas_call x1, Pallas kernels, attend_resident(): pl.pallas_call(resident_kernel, grid_spec=pltpu.PrefetchScalarGridSpec(nu...  13.5 us
    all_to_all x2, starting transfers between devices, exchange(): out = lax.all_to_all(split, 'rep', split_axis=0, concat_axis=0, tiled=True)  10.9 us
    all_to_all x2, waiting for transfers between devices, exchange(): out = lax.all_to_all(split, 'rep', split_axis=0, concat_axis=0, tiled=True)  8.47 us
    pallas_call x1, Pallas kernels, update_late(): pl.pallas_call(late_kernel, grid_spec=pltpu.PrefetchScalarGridSpec(num_sc...  7.14 us
    pallas_call x1, Pallas kernels, update_early(): pl.pallas_call(functools.partial(early_kernel, late), grid_spec=pltpu.Pre...  5.99 us
    pallas_call x1, Pallas kernels, attend_paged(): pl.pallas_call(paged_kernel, grid_spec=pltpu.PrefetchScalarGridSpec(num_s...  5.75 us
  transfers between devices with their start and end apart: 2, of which 1 were waited for; matrix products, arithmetic and copies ran while one was open for 5% of the time, Pallas kernels for 52%

profile of v2, /device:TPU:0, one launch (start us, length us, event | category | flops | bytes accessed | tf_op | source)
XLA Modules:
  0.0 101.9 jit_solution(2557170950317267784)
XLA Ops:
  0.6 0.8 copy.37
  1.4 0.1 broadcast_in_dim_reshape_squeeze.3.slot_ref
  1.5 0.9 copy-done.10
  2.4 1.0 copy-done.12
  3.4 0.8 copy-done.15
  4.1 0.7 copy-done.21
  4.8 0.7 copy-done.23
  5.4 0.3 ask.1
  5.8 1.0 reshape.44
  6.7 7.2 %all-to-all-start = ((bf16[8,2,14848]{2,1,0:T(2,128)(2,1)}), bf16[8,2,14848]{2,1,0:T(2,128)(2,1)S(1)}, u32[]{:S(2)}, u32[]{:S(2)}) async-start(bf16[8,2,14848]{2,1,0:T(2,128)(2,1)} %reshape.44), calls=%async_computation | async-start | bytes 950272 | tf_op jit(solution)/shard_map/all_to_all | solution.py:592
  14.0 0.1 reshape_squeeze.9.slots
  14.0 3.5 %pack_states.1 = bf16[16,16,4096]{2,1,0:T(8,128)(2,1)S(1)} custom-call(s32[16]{0:T(128)S(1)} %reshape_squeeze.9.slots, f32[16,16,4096]{2,1,0:T(8,128)} %refs_3_.3, f32[16,16,4096]{2,1,0:T(8,128)} %refs_3_.3, f32[16,16,4096]{2,1,0:T(8,128)} %refs_3_.3, f32[16,16,4096]{2,1,0:T(8,128)} %refs_3_.3), custom_call_target="tpu_custom_call" | custom-call | bytes 6291456 | tf_op jit(solution)/shard_map/pack_states/pallas_call | solution.py:169
  17.5 0.0 copy-start
  17.6 1.3 %copy-done = bf16[16,16,4096]{2,1,0:T(8,128)(2,1)} copy-done((bf16[16,16,4096]{2,1,0:T(8,128)(2,1)}, bf16[16,16,4096]{2,1,0:T(8,128)(2,1)S(1)}, u32[]{:S(2)}) %copy-start) | copy-done | bytes 2097176
  18.9 0.0 copy-start.26
  18.9 8.5 %all-to-all-done = bf16[8,2,14848]{2,1,0:T(2,128)(2,1)S(1)} async-done(((bf16[8,2,14848]{2,1,0:T(2,128)(2,1)}), bf16[8,2,14848]{2,1,0:T(2,128)(2,1)S(1)}, u32[]{:S(2)}, u32[]{:S(2)}) %all-to-all-start) | async-done | bytes 475168 | tf_op jit(solution)/shard_map/all_to_all | solution.py:592
  27.4 0.2 reshape.45.got_ref
  27.6 3.6 %all-to-all-start.1 = ((bf16[8,2,16,4096]{3,2,1,0:T(8,128)(2,1)}), bf16[8,2,16,4096]{3,2,1,0:T(8,128)(2,1)S(1)}, u32[]{:S(2)}, u32[]{:S(2)}) async-start(bf16[8,2,16,4096]{3,2,1,0:T(8,128)(2,1)} %bitcast.32), calls=%async_computation.1 | async-start | bytes 4194304 | tf_op jit(solution)/shard_map/all_to_all | solution.py:592
  31.2 0.0 copy-done.16
  31.3 0.0 copy-done.31
  31.3 0.1 copy.39
  31.3 0.1 reshape_squeeze.10.lens
  31.4 0.0 copy-done.30
  31.4 0.1 reshape_squeeze.11.pages
  31.5 0.0 copy-done.11
  31.5 0.0 copy-done.26
  31.6 0.0 copy-start.22
  31.6 0.0 copy-start.24
  31.6 13.5 %attend_resident.1 = bf16[32,16,128]{2,1,0:T(8,128)(2,1)S(1)} custom-call(s32[32]{0:T(128)S(1)} %copy-done.26, bf16[32,16,128]{2,1,0:T(8,128)(2,1)S(1)} %bitcast.35, bf16[32,512,512]{2,1,0:T(8,128)(2,1)} %kv_ref.1, bf16[32,4,128]{2,1,0:T(4,128)(2,1)S(1)} %reshape.53.nkv_ref), custom_call_target="tpu_custom_call" | custom-call | flops 268435456 | bytes 16777216 | tf_op jit(solution)/shard_map/attend_resident/pallas_call | solution.py:106
  45.1 0.0 copy-done.22
  45.1 0.0 copy-done.24
  45.1 0.0 copy-start.17
  45.1 0.0 copy-start.18
  45.2 0.6 broadcast_maximum_fusion
  45.8 0.6 pad_clamp_fusion
  46.4 0.2 convert_reduce_fusion
  46.6 0.7 add_select_fusion
  47.2 0.1 select_reduce_fusion.perm
  47.4 0.0 copy-done.32
  47.4 0.0 copy-start.1
  47.4 2.2 %copy-done.1 = bf16[256,16,512]{2,1,0:T(8,128)(2,1)S(1)} copy-done((bf16[256,16,512]{2,1,0:T(8,128)(2,1)S(1)}, bf16[256,16,512]{2,1,0:T(8,128)(2,1)}, u32[]{:S(2)}) %copy-start.1) | copy-done | bytes 4194328
  49.6 0.0 copy-start.28
  49.6 5.7 %attend_paged.1 = bf16[16,16,128]{2,1,0:T(8,128)(2,1)S(1)} custom-call(s32[16]{0:T(128)S(1)} %reshape_squeeze.10.lens, s32[512]{0:T(512)S(1)} %reshape_squeeze.11.pages, bf16[16,16,128]{2,1,0:T(8,128)(2,1)S(1)} %bitcast.39, bf16[256,16,512]{2,1,0:T(8,128)(2,1)S(1)} %copy-done.1, bf16[16,4,128]{2,1,0:T(4,128)(2,1)S(1)} %reshape.49.nkv_ref), custom_call_target="tpu_custom_call" | custom-call | flops 134217728 | bytes 4194304 | tf_op jit(solution)/shard_map/attend_paged/pallas_call | solution.py:132
  55.4 0.0 copy-done.17
  55.4 0.0 copy-done.18
  55.4 0.0 copy-start.7
  55.4 1.1 %copy-done.7 = bf16[32,3,4096]{2,0,1:T(8,128)(2,1)S(1)} copy-done((bf16[32,3,4096]{2,0,1:T(8,128)(2,1)S(1)}, bf16[32,3,4096]{2,0,1:T(8,128)(2,1)}, u32[]{:S(2)}) %copy-start.7) | copy-done | bytes 786456
  56.5 0.9 copy-done.14
  57.5 4.2 %conv_proj.1 = (f32[32,4096]{1,0:T(8,128)S(1)}, bf16[3,32,4096]{2,1,0:T(8,128)(2,1)}, f32[32,544]{1,0:T(8,128)S(1)}) custom-call(s32[1,32]{1,0:T(1,128)S(1)} %bitcast.45, s32[1,32]{1,0:T(1,128)S(1)} %bitcast.47, bf16[32,4096]{1,0:T(8,128)(2,1)S(1)} %copy-done.14, bf16[3,32,4096]{2,1,0:T(8,128)(2,1)S(1)} %bitcast.33, bf16[16,14848]{1,0:T(8,128)(2,1)S(1)} %reshape.45.got_ref, ...), custom_call_target="tpu_custom_call" | custom-call | flops 142606336 | bytes 6553600 | tf_op jit(solution)/shard_map/conv_proj/pallas_call | solution.py:266
  61.7 0.0 copy-done.2
  61.7 20.1 %tp_sum_step.1 = (f32[32,4096]{1,0:T(8,128)S(1)}, f32[2,32,16]{2,1,0:T(8,128)S(1)}, bf16[8,2,16,128]{3,2,1,0:T(8,128)(2,1)S(1)}) custom-call(f32[32,544]{1,0:T(8,128)S(1)} %get-tuple-element.18.part_ref, bf16[8,2,16,128]{3,2,1,0:T(8,128)(2,1)S(1)} %bitcast.38, bf16[512,4096]{1,0:T(8,128)(2,1)S(1)} %copy-done.2, f32[1,4096]{1,0:T(1,128)S(1)} %bitcast.42, ...), custom_call_target="tpu_custom_call" | custom-call | flops 134217728 | bytes 4718592 | tf_op jit(solution)/shard_map/tp_sum_step/pallas_call | solution.py:345
  81.9 0.8 copy-done.3
  82.7 1.4 %gather_fusion = bf16[32,2048]{1,0:T(8,128)(2,1)} fusion(bf16[16,2048]{1,0:T(8,128)(2,1)S(1)} %bitcast.51, s32[1024]{0:T(1024)} %pad_clamp_fusion), kind=kCustom, calls=%fused_computation | custom fusion | bytes 262272 | tf_op jit(solution)/shard_map/jit(_take)/gather | solution.py:629
  84.1 0.0 copy-done.6
  84.1 1.0 %copy-done.4 = f32[32,4096]{1,0:T(8,128)S(1)} copy-done((f32[32,4096]{1,0:T(8,128)S(1)}, f32[32,4096]{1,0:T(8,128)}, u32[]{:S(2)}) %copy-start.4) | copy-done | bytes 524312
  85.2 6.0 %ssm_early.1 = (f32[32,16,4096]{2,1,0:T(8,128)}, f32[32,4096]{1,0:T(8,128)S(1)}) custom-call(s32[32]{0:T(128)S(1)} %select_reduce_fusion.perm, f32[32,16,4096]{2,1,0:T(8,128)} %refs_3_.5, f32[32,16,4096]{2,1,0:T(8,128)} %refs_3_.5, f32[32,16,4096]{2,1,0:T(8,128)} %refs_3_.5, f32[32,16,4096]{2,1,0:T(8,128)} %refs_3_.5, f32[32,4096]{1,0:T(8,128)S(1)} %copy-done.4, ...), custom_call_target="tpu_custom_call" | custom-call | flops 8388608 | bytes 8388608 | tf_op jit(solution)/shard_map/ssm_early/pallas_call | solution.py:474
  91.2 0.0 copy-start.8
  91.2 0.8 copy-done.8
  92.0 0.7 bitcast_select_fusion
  92.7 0.0 all-to-all-done.1
  92.7 0.0 copy-done.13
  92.7 1.0 %copy-done.5 = f32[32,4096]{1,0:T(8,128)S(1)} copy-done((f32[32,4096]{1,0:T(8,128)S(1)}, f32[32,4096]{1,0:T(8,128)}, u32[]{:S(2)}) %copy-start.5) | copy-done | bytes 524312
  93.7 1.0 %copy-done.9 = f32[32,4096]{1,0:T(8,128)S(1)} copy-done((f32[32,4096]{1,0:T(8,128)S(1)}, f32[32,4096]{1,0:T(8,128)}, u32[]{:S(2)}) %copy-start.9) | copy-done | bytes 524312
  94.8 7.1 %ssm_late.1 = (f32[32,16,4096]{2,1,0:T(8,128)}, bf16[32,4096]{1,0:T(8,128)(2,1)}) custom-call(s32[32]{0:T(128)S(1)} %select_reduce_fusion.perm, s32[32]{0:T(128)S(1)} %get-tuple-element.29.source, f32[32,16,4096]{2,1,0:T(8,128)} %refs_3_.5, f32[32,16,4096]{2,1,0:T(8,128)} %refs_3_.5, f32[32,16,4096]{2,1,0:T(8,128)} %refs_3_.5, ...), custom_call_target="tpu_custom_call", output_to_operand_aliasing={{0}: (17, {})} | custom-call | flops 8388608 | bytes 10485760 | tf_op jit(solution)/shard_map/ssm_late/pallas_call | solution.py:513
  (39 shorter events, 0.1 us)
Async XLA Ops:
  1.5 0.9 copy-start.10
  2.4 1.0 copy-start.12
  3.4 0.8 copy-start.15
  4.1 0.7 copy-start.21
  4.8 0.7 copy-start.23
  6.7 20.7 %all-to-all-start = ((bf16[8,2,14848]{2,1,0:T(2,128)(2,1)}), bf16[8,2,14848]{2,1,0:T(2,128)(2,1)S(1)}, u32[]{:S(2)}, u32[]{:S(2)}) async-start(bf16[8,2,14848]{2,1,0:T(2,128)(2,1)} %reshape.44), calls=%async_computation | async-start | bytes 950272 | tf_op jit(solution)/shard_map/all_to_all | solution.py:592
  17.5 1.4 %copy-start = (bf16[16,16,4096]{2,1,0:T(8,128)(2,1)}, bf16[16,16,4096]{2,1,0:T(8,128)(2,1)S(1)}, u32[]{:S(2)}) copy-start(bf16[16,16,4096]{2,1,0:T(8,128)(2,1)S(1)} %pack_states.1) | copy-start | bytes 6291460
  18.9 12.3 %copy-start.16 = (bf16[32,512]{1,0:T(8,128)(2,1)S(1)}, bf16[32,512]{1,0:T(8,128)(2,1)}, u32[]{:S(2)}) copy-start(bf16[32,512]{1,0:T(8,128)(2,1)} %new_ref.1) | copy-start | bytes 98308
  18.9 12.4 %copy-start.31 = (s32[1,8,2]{1,2,0:T(2,128)S(1)}, s32[1,8,2]{1,2,0:T(2,128)}, u32[]{:S(2)}) copy-start(s32[1,8,2]{1,2,0:T(2,128)} %param.50) | copy-start | bytes 196
  18.9 12.5 %copy-start.30 = (s32[1,8,2,32]{3,2,1,0:T(2,128)S(1)}, s32[1,8,2,32]{3,2,1,0:T(2,128)}, u32[]{:S(2)}) copy-start(s32[1,8,2,32]{3,2,1,0:T(2,128)} %param.51) | copy-start | bytes 6148
  18.9 12.6 %copy-start.11 = (bf16[32,2048]{1,0:T(8,128)(2,1)S(1)}, bf16[32,2048]{1,0:T(8,128)(2,1)}, u32[]{:S(2)}) copy-start(bf16[32,2048]{1,0:T(8,128)(2,1)} %query_ref.1) | copy-start | bytes 393220
  18.9 12.6 %copy-start.26 = (s32[32]{0:T(128)S(1)}, s32[32]{0:T(128)}, u32[]{:S(2)}) copy-start(s32[32]{0:T(128)} %lens.1) | copy-start | bytes 388
  27.6 65.1 %all-to-all-start.1 = ((bf16[8,2,16,4096]{3,2,1,0:T(8,128)(2,1)}), bf16[8,2,16,4096]{3,2,1,0:T(8,128)(2,1)S(1)}, u32[]{:S(2)}, u32[]{:S(2)}) async-start(bf16[8,2,16,4096]{3,2,1,0:T(8,128)(2,1)} %bitcast.32), calls=%async_computation.1 | async-start | bytes 4194304 | tf_op jit(solution)/shard_map/all_to_all | solution.py:592
  31.6 13.6 %copy-start.22 = (s32[32]{0:T(128)S(1)}, s32[32]{0:T(128)}, u32[]{:S(2)}) copy-start(s32[32]{0:T(128)} %param.47) | copy-start | bytes 388
  31.6 13.6 %copy-start.24 = (s32[32]{0:T(128)S(1)}, s32[32]{0:T(128)}, u32[]{:S(2)}) copy-start(s32[32]{0:T(128)} %param.48) | copy-start | bytes 388
  45.1 10.3 %copy-start.17 = (bf16[4,4096]{1,0:T(4,128)(2,1)S(1)}, bf16[4,4096]{1,0:T(4,128)(2,1)}, u32[]{:S(2)}) copy-start(bf16[4,4096]{1,0:T(4,128)(2,1)} %weight_ref.1) | copy-start | bytes 98308
  45.1 10.3 %copy-start.18 = (f32[4096]{0:T(1024)S(1)}, f32[4096]{0:T(1024)}, u32[]{:S(2)}) copy-start(f32[4096]{0:T(1024)} %param.33) | copy-start | bytes 49156
  46.4 1.0 copy-start.32
  47.4 2.2 %copy-start.1 = (bf16[256,16,512]{2,1,0:T(8,128)(2,1)S(1)}, bf16[256,16,512]{2,1,0:T(8,128)(2,1)}, u32[]{:S(2)}) copy-start(bf16[256,16,512]{2,1,0:T(8,128)(2,1)} %pool_ref.1) | copy-start | bytes 12582916
  49.6 12.1 %copy-start.2 = (bf16[512,4096]{1,0:T(8,128)(2,1)S(1)}, bf16[512,4096]{1,0:T(8,128)(2,1)}, u32[]{:S(2)}) copy-start(bf16[512,4096]{1,0:T(8,128)(2,1)} %dt_proj_ref.1) | copy-start | bytes 12582916
  49.6 12.1 %copy-start.19 = (f32[4096]{0:T(1024)S(1)}, f32[4096]{0:T(1024)}, u32[]{:S(2)}) copy-start(f32[4096]{0:T(1024)} %param.39) | copy-start | bytes 49156
  49.6 12.1 %copy-start.25 = (f32[512]{0:T(512)S(1)}, f32[512]{0:T(512)}, u32[]{:S(2)}) copy-start(f32[512]{0:T(512)} %param.35) | copy-start | bytes 6148
  49.6 12.1 %copy-start.27 = (f32[16]{0:T(128)S(1)}, f32[16]{0:T(128)}, u32[]{:S(2)}) copy-start(f32[16]{0:T(128)} %param.36) | copy-start | bytes 196
  49.6 12.1 %copy-start.28 = (f32[16]{0:T(128)S(1)}, f32[16]{0:T(128)}, u32[]{:S(2)}) copy-start(f32[16]{0:T(128)} %param.37) | copy-start | bytes 196
  55.4 1.1 %copy-start.7 = (bf16[32,3,4096]{2,0,1:T(8,128)(2,1)S(1)}, bf16[32,3,4096]{2,0,1:T(8,128)(2,1)}, u32[]{:S(2)}) copy-start(bf16[32,3,4096]{2,0,1:T(8,128)(2,1)} %param.28) | copy-start | bytes 2359300
  56.5 0.9 copy-start.14
  57.5 26.6 %copy-start.6 = (f32[16,4096]{1,0:T(8,128)S(1)}, f32[16,4096]{1,0:T(8,128)}, u32[]{:S(2)}) copy-start(f32[16,4096]{1,0:T(8,128)} %refs_11_.1) | copy-start | bytes 786436
  81.8 0.8 copy-start.3
  84.1 1.0 %copy-start.4 = (f32[32,4096]{1,0:T(8,128)S(1)}, f32[32,4096]{1,0:T(8,128)}, u32[]{:S(2)}) copy-start(f32[32,4096]{1,0:T(8,128)} %copy-done.3) | copy-start | bytes 1572868
  85.1 6.8 %copy-start.29 = (bf16[32,2048]{1,0:T(8,128)(2,1)S(1)}, bf16[32,2048]{1,0:T(8,128)(2,1)}, u32[]{:S(2)}) copy-start(bf16[32,2048]{1,0:T(8,128)(2,1)} %gather_fusion) | copy-start | bytes 393220
  85.1 6.8 %copy-start.33 = (pred[32]{0:T(512)(128)(4,1)S(1)}, pred[32]{0:T(512)(128)(4,1)}, u32[]{:S(2)}) copy-start(pred[32]{0:T(512)(128)(4,1)} %copy-done.32) | copy-start | bytes 100
  85.2 7.5 %copy-start.13 = (bf16[32,4096]{1,0:T(8,128)(2,1)S(1)}, bf16[32,4096]{1,0:T(8,128)(2,1)}, u32[]{:S(2)}) copy-start(bf16[32,4096]{1,0:T(8,128)(2,1)} %refs_14_.1) | copy-start | bytes 786436
  85.2 7.5 %copy-start.20 = (f32[4096]{0:T(1024)S(1)}, f32[4096]{0:T(1024)}, u32[]{:S(2)}) copy-start(f32[4096]{0:T(1024)} %param.41) | copy-start | bytes 49156
  91.2 0.8 copy-start.8
  92.7 1.0 %copy-start.5 = (f32[32,4096]{1,0:T(8,128)S(1)}, f32[32,4096]{1,0:T(8,128)}, u32[]{:S(2)}) copy-start(f32[32,4096]{1,0:T(8,128)} %copy-done.3) | copy-start | bytes 1572868
  93.7 1.0 %copy-start.9 = (f32[32,4096]{1,0:T(8,128)S(1)}, f32[32,4096]{1,0:T(8,128)}, u32[]{:S(2)}) copy-start(f32[32,4096]{1,0:T(8,128)} %copy-done.8) | copy-start | bytes 1572868

commit v3 on v2

--- a/solution.py
+++ b/solution.py
@@ -153,36 +153,6 @@
     )(lens, pages, q, pool, nkv)
 
 
-def pack_kernel(slots, *refs):
-    out_ref = refs[-1]
-    for k, ref in enumerate(refs[:-1]):
-        out_ref[k] = ref[0].astype(jnp.bfloat16)
-
-
-def pack_states(pool, slots):
-    entries = slots.shape[0]
-    block = (1,) + pool.shape[1:]
-
-    def spec(k):
-        return pl.BlockSpec(block, lambda i, slots: (slots[i * BATCH + k], 0, 0))
-
-    return pl.pallas_call(
-        pack_kernel,
-        grid_spec=pltpu.PrefetchScalarGridSpec(
-            num_scalar_prefetch=1,
-            grid=(entries // BATCH,),
-            in_specs=[spec(k) for k in range(BATCH)],
-            out_specs=pl.BlockSpec((BATCH,) + pool.shape[1:], lambda i, slots: (i, 0, 0)),
-        ),
-        out_shape=jax.ShapeDtypeStruct((entries,) + pool.shape[1:], jnp.bfloat16),
-        compiler_params=params(),
-        cost_estimate=pl.CostEstimate(
-            flops=0, bytes_accessed=6 * entries * pool[0].size, transcendentals=0
-        ),
-        name="pack_states",
-    )(slots, *([pool] * BATCH))
-
-
 def entry_match(owner_ref, pos_ref, entries, cap):
     owner = owner_ref[...]
     source = jnp.where(owner >= 0, owner * cap + pos_ref[...], -1)
@@ -197,39 +167,154 @@
     )
 
 
-def ask_kernel(cap, owner_ref, pos_ref, slot_ref, pool_ref, query_ref, new_ref, out_ref):
+def greet(partners):
+    barrier = pltpu.get_barrier_semaphore()
+    for partner in partners:
+        pl.semaphore_signal(barrier, inc=1, device_id=partner, device_id_type=MESH)
+    return lambda: pl.semaphore_wait(barrier, len(partners))
+
+
+def trade_kernel(peers, cap, slots_ref, owner_hbm, pos_hbm, line_hbm, pool_hbm, query_hbm, new_hbm,
+                 states_hbm, got_ref, packed_ref, owner_ref, pos_ref, line_ref, pool_ref,
+                 query_ref, new_ref, states_ref, send_ref, load_sem, own_sem, send_sem, recv_sem):
+    group = lax.axis_index("rep")
+    others = [lax.rem(group + k, peers) for k in range(1, peers)]
+    wait_greetings = greet([{"rep": other} for other in others])
     taps, slots, channels = pool_ref.shape
-    entries = out_ref.shape[0]
+    entries = peers * cap
+    loads = [
+        pltpu.make_async_copy(src, dst, load_sem.at[k])
+        for k, (src, dst) in enumerate(
+            (
+                (owner_hbm, owner_ref),
+                (pos_hbm, pos_ref),
+                (line_hbm, line_ref),
+                (pool_hbm, pool_ref),
+                (query_hbm, query_ref),
+                (new_hbm, new_ref),
+                (states_hbm, states_ref),
+            )
+        )
+    ]
+    for load in loads:
+        load.start()
+    for load in loads[:-1]:
+        load.wait()
+
+    def put(rows, at):
+        for p in range(peers):
+            send_ref[p, :, at : at + rows.shape[1]] = rows[p * cap : (p + 1) * cap].astype(
+                jnp.bfloat16
+            )
+
     shape = (slots, entries)
-    hit = lax.broadcasted_iota(jnp.int32, shape, 0) == jnp.broadcast_to(slot_ref[...], shape)
+    hit = lax.broadcasted_iota(jnp.int32, shape, 0) == jnp.broadcast_to(line_ref[...], shape)
     chosen = jnp.where(hit, 1.0, 0.0).astype(jnp.bfloat16)
     for j in range(taps):
-        out_ref[:, j * channels : (j + 1) * channels] = pick(chosen, pool_ref[j], 0).astype(
-            jnp.bfloat16
-        )
+        put(pick(chosen, pool_ref[j], 0), j * channels)
     match = entry_match(owner_ref, pos_ref, entries, cap)
     at = taps * channels
     for ref in (query_ref, new_ref):
-        out_ref[:, at : at + ref.shape[1]] = pick(match, ref[...], 1).astype(jnp.bfloat16)
+        put(pick(match, ref[...], 1), at)
         at += ref.shape[1]
 
-
-def ask(cap, owner, pos, slots, pool, query, new_kv):
-    entries = slots.shape[1]
-    operands = (owner, pos, slots, pool, query, new_kv)
+    wait_greetings()
+    copies = []
+    for k, other in enumerate(others):
+        copy = pltpu.make_async_remote_copy(
+            src_ref=send_ref.at[other],
+            dst_ref=got_ref.at[group],
+            send_sem=send_sem.at[k],
+            recv_sem=recv_sem.at[k],
+            device_id={"rep": other},
+            device_id_type=MESH,
+        )
+        copy.start()
+        copies.append(copy)
+    own = pltpu.make_async_copy(send_ref.at[group], got_ref.at[group], own_sem)
+    own.start()
+    loads[-1].wait()
+
+    def pack(e, carry):
+        packed_ref[e] = states_ref[slots_ref[e]].astype(jnp.bfloat16)
+        return carry
+
+    lax.fori_loop(0, entries, pack, 0)
+    own.wait()
+    for copy in copies:
+        copy.wait()
+
+
+def trade(peers, cap, slots, owner, pos, pool, query, new_kv, states):
+    entries = slots.shape[0]
     width = pool.shape[0] * pool.shape[2] + query.shape[1] + new_kv.shape[1]
+    anywhere = pl.BlockSpec(memory_space=pl.ANY)
+    operands = (owner, pos, slots[None, :], pool, query, new_kv, states)
     return pl.pallas_call(
-        functools.partial(ask_kernel, cap),
-        grid=(1,),
-        in_specs=[whole(a.shape) for a in operands],
-        out_specs=whole((entries, width)),
-        out_shape=jax.ShapeDtypeStruct((entries, width), jnp.bfloat16),
-        compiler_params=params(),
+        functools.partial(trade_kernel, peers, cap),
+        in_specs=[pl.BlockSpec(memory_space=pltpu.SMEM)] + [anywhere] * len(operands),
+        out_specs=(anywhere, pl.BlockSpec(memory_space=pltpu.VMEM)),
+        out_shape=(
+            jax.ShapeDtypeStruct((peers, cap, width), jnp.bfloat16),
+            jax.ShapeDtypeStruct((entries,) + states.shape[1:], jnp.bfloat16),
+        ),
+        scratch_shapes=[pltpu.VMEM(a.shape, a.dtype) for a in operands]
+        + [
+            pltpu.VMEM((peers, cap, width), jnp.bfloat16),
+            pltpu.SemaphoreType.DMA((len(operands),)),
+            pltpu.SemaphoreType.DMA,
+            pltpu.SemaphoreType.DMA((peers - 1,)),
+            pltpu.SemaphoreType.DMA((peers - 1,)),
+        ],
+        compiler_params=params(collective_id=1, has_side_effects=True),
         cost_estimate=pl.CostEstimate(
-            flops=2 * entries * pool.size, bytes_accessed=4 * pool.size, transcendentals=0
-        ),
-        name="ask",
-    )(*operands)
+            flops=2 * entries * pool.size, bytes_accessed=6 * states.size, transcendentals=0
+        ),
+        name="trade",
+    )(slots, *operands)
+
+
+def home_kernel(peers, attn_ref, back_ref, home_ref, send_sem, recv_sem):
+    group = lax.axis_index("rep")
+    homes = [lax.rem(group + k, peers) for k in range(1, peers)]
+    greet([{"rep": home} for home in homes])()
+    copies = []
+    for k, home in enumerate(homes):
+        copy = pltpu.make_async_remote_copy(
+            src_ref=attn_ref.at[home],
+            dst_ref=home_ref.at[k],
+            send_sem=send_sem.at[k],
+            recv_sem=recv_sem.at[k],
+            device_id={"rep": home},
+            device_id_type=MESH,
+        )
+        copy.start()
+        copies.append(copy)
+    back_ref[group] = attn_ref[group]
+    for k, copy in enumerate(copies):
+        copy.wait_recv()
+        back_ref[lax.rem(group + peers - 1 - k, peers)] = home_ref[k]
+    for copy in copies:
+        copy.wait_send()
+
+
+def send_home(attn):
+    peers = attn.shape[0]
+    vmem = pl.BlockSpec(memory_space=pltpu.VMEM)
+    return pl.pallas_call(
+        functools.partial(home_kernel, peers),
+        out_shape=jax.ShapeDtypeStruct(attn.shape, jnp.bfloat16),
+        in_specs=[vmem],
+        out_specs=vmem,
+        scratch_shapes=[
+            pltpu.VMEM((peers - 1,) + attn.shape[1:], jnp.bfloat16),
+            pltpu.SemaphoreType.DMA((peers - 1,)),
+            pltpu.SemaphoreType.DMA((peers - 1,)),
+        ],
+        compiler_params=params(collective_id=2, has_side_effects=True),
+        cost_estimate=pl.CostEstimate(flops=0, bytes_accessed=4 * attn.size, transcendentals=0),
+        name="send_home",
+    )(attn)
 
 
 def conv_kernel(cap, owner_ref, pos_ref, x_ref, state_ref, got_ref, weight_ref, bias_ref,
@@ -278,17 +363,11 @@
     )(*operands)
 
 
-def step_kernel(count, peers, part_ref, attn_ref, dt_proj_ref, bias_ref, dt_gain_ref, b_gain_ref,
-                c_gain_ref, dt_ref, bc_ref, back_ref, got_ref, home_ref, send_sem, recv_sem,
-                home_send, home_recv):
+def step_kernel(count, part_ref, dt_proj_ref, bias_ref, dt_gain_ref, b_gain_ref, c_gain_ref,
+                dt_ref, bc_ref, got_ref, send_sem, recv_sem):
     me = lax.axis_index("tp")
-    group = lax.axis_index("rep")
-    barrier = pltpu.get_barrier_semaphore()
     partners = [{"tp": lax.rem(me + k, count)} for k in range(1, count)]
-    homes = [lax.rem(group + k, peers) for k in range(1, peers)]
-    for partner in partners + [{"rep": home} for home in homes]:
-        pl.semaphore_signal(barrier, inc=1, device_id=partner, device_id_type=MESH)
-    pl.semaphore_wait(barrier, count + peers - 2)
+    greet(partners)()
     copies = []
     for k, partner in enumerate(partners):
         copy = pltpu.make_async_remote_copy(
@@ -301,18 +380,6 @@
         )
         copy.start()
         copies.append(copy)
-    returns = []
-    for k, home in enumerate(homes):
-        copy = pltpu.make_async_remote_copy(
-            src_ref=attn_ref.at[home],
-            dst_ref=home_ref.at[k],
-            send_sem=home_send.at[k],
-            recv_sem=home_recv.at[k],
-            device_id={"rep": home},
-            device_id_type=MESH,
-        )
-        copy.start()
-        returns.append(copy)
     proj = part_ref[...]
     for k, copy in enumerate(copies):
         copy.wait_recv()
@@ -329,35 +396,26 @@
     dt_ref[...] = jnp.maximum(raw, 0.0) + jnp.log1p(jnp.exp(-jnp.abs(raw)))
     bc_ref[0] = rms_scaled(proj[:, rank : rank + states], b_gain_ref[...]).astype(jnp.float32)
     bc_ref[1] = rms_scaled(proj[:, rank + states :], c_gain_ref[...]).astype(jnp.float32)
-    back_ref[group] = attn_ref[group]
-    for k, copy in enumerate(returns):
-        copy.wait_recv()
-        back_ref[lax.rem(group + peers - 1 - k, peers)] = home_ref[k]
-    for copy in copies + returns:
+    for copy in copies:
         copy.wait_send()
 
 
-def step_sizes(count, part, attn, dt_proj, dt_bias, dt_gain, b_gain, c_gain):
+def step_sizes(count, part, dt_proj, dt_bias, dt_gain, b_gain, c_gain):
     rows = part.shape[0]
-    peers = attn.shape[0]
     channels = dt_proj.shape[1]
     vmem = pl.BlockSpec(memory_space=pltpu.VMEM)
     return pl.pallas_call(
-        functools.partial(step_kernel, count, peers),
+        functools.partial(step_kernel, count),
         out_shape=(
             jax.ShapeDtypeStruct((rows, channels), jnp.float32),
             jax.ShapeDtypeStruct((2, rows, b_gain.shape[1]), jnp.float32),
-            jax.ShapeDtypeStruct(attn.shape, jnp.bfloat16),
-        ),
-        in_specs=[vmem] * 7,
-        out_specs=(vmem, vmem, vmem),
+        ),
+        in_specs=[vmem] * 6,
+        out_specs=(vmem, vmem),
         scratch_shapes=[
             pltpu.VMEM((count - 1,) + part.shape, jnp.float32),
-            pltpu.VMEM((peers - 1,) + attn.shape[1:], jnp.bfloat16),
             pltpu.SemaphoreType.DMA((count - 1,)),
             pltpu.SemaphoreType.DMA((count - 1,)),
-            pltpu.SemaphoreType.DMA((peers - 1,)),
-            pltpu.SemaphoreType.DMA((peers - 1,)),
         ],
         compiler_params=params(collective_id=0, has_side_effects=True),
         cost_estimate=pl.CostEstimate(
@@ -365,7 +423,7 @@
             transcendentals=2 * rows * channels,
         ),
         name="tp_sum_step",
-    )(part, attn, dt_proj, dt_bias, dt_gain, b_gain, c_gain)
+    )(part, dt_proj, dt_bias, dt_gain, b_gain, c_gain)
 
 
 def update_row(row, prev, dt_ref, signal_ref, bc_ref, decay_ref):
@@ -587,21 +645,16 @@
         jnp.where(place[None, :] == row_ids[:, None], row_ids[None, :], 0), axis=1
     ).astype(jnp.int32)
 
-    def exchange(block):
-        split = block.reshape((peer_count, slot_cap) + block.shape[1:])
-        out = lax.all_to_all(split, "rep", split_axis=0, concat_axis=0, tiled=True)
-        return out.reshape(block.shape)
-
     owner_line, pos_line = row_owner[None, :], row_pos[None, :]
-    first = exchange(
-        ask(
-            slot_cap, owner_line, pos_line, slot_list[None, :], jnp.swapaxes(conv_pool, 0, 1),
-            query, new_kv,
-        )
-    )
-    states = pack_states(ssm_pool, slot_list)
-    first, states = lax.optimization_barrier((first, states))
-    states_in = exchange(states)
+    first, states = trade(
+        peer_count, slot_cap, slot_list, owner_line, pos_line, jnp.swapaxes(conv_pool, 0, 1),
+        query, new_kv, ssm_pool,
+    )
+    first = first.reshape(entry_count, -1)
+    states_in = lax.all_to_all(
+        states.reshape((peer_count, slot_cap) + states.shape[1:]), "rep", split_axis=0,
+        concat_axis=0, tiled=True,
+    ).reshape(states.shape)
 
     query_rows = query.reshape(row_count, head_count, HD)
     new_rows = new_kv.reshape(row_count, -1, HD)
@@ -621,19 +674,21 @@
         query_in, kv_pool, new_in, swap_lens[0].reshape(-1), swap_pages[0].reshape(-1),
         kv_cache.shape[1],
     )
-    dt_step, bc, attn_back = step_sizes(
-        tp_count, part, attn_there.reshape(peer_count, slot_cap, head_count, HD), dt_proj,
-        dt_bias[None, :], dt_gain[None, :], b_gain[None, :], c_gain[None, :],
-    )
-    attn_back = attn_back.reshape(entry_count, query_width)
-    picked = jnp.take(attn_back, jnp.maximum(source, 0), axis=0, mode="clip")
-    attn_out = jnp.where(resumed[:, None], picked, attn_here)
-
+    dt_step, bc = step_sizes(
+        tp_count, part, dt_proj, dt_bias[None, :], dt_gain[None, :], b_gain[None, :],
+        c_gain[None, :],
+    )
     late = min(row_count, entry_count)
     if late < row_count:
         kept, early_y = update_early(perm, ssm_state, dt_step, mixed, bc, decay_rate, late)
     else:
         kept, early_y = jnp.zeros_like(ssm_state), jnp.zeros_like(dt_step)
+    attn_there, early_y = lax.optimization_barrier((attn_there, early_y))
+    attn_back = send_home(attn_there.reshape(peer_count, slot_cap, head_count, HD))
+    attn_back, early_y = lax.optimization_barrier((attn_back, early_y))
+    attn_back = attn_back.reshape(entry_count, query_width)
+    picked = jnp.take(attn_back, jnp.maximum(source, 0), axis=0, mode="clip")
+    attn_out = jnp.where(resumed[:, None], picked, attn_here)
     new_ssm, mamba_out = update_late(
         perm, source, ssm_state, states_in, dt_step, mixed, bc, decay_rate, early_y,
         skip[None, :], z_gate, kept, late,

time: 103 us -> 104 us (level)
  Pallas kernels: 60.5 us -> 78.1 us
  waiting for transfers between devices: 8.47 us -> 0.01 us
  local copies, waits for them, and re-layouts: 18.2 us -> 14.4 us
  starting transfers between devices: 10.9 us -> 7.66 us
    pallas_call x3, Pallas kernels: 23.9 us -> 41.3 us  [the longest x1 20.2 us: send_home(): pl.pallas_call(functools.partial(home_kernel, peers), out_shape=jax.Shape...]
    all_to_all x2 -> x1, waiting for transfers between devices: 8.47 us -> 0.01 us  [shards(): lax.all_to_all(states.reshape((peer_count, slot_cap) + states.shape[1:]),...]
    all_to_all x2 -> x1, starting transfers between devices: 10.9 us -> 7.66 us  [shards(): lax.all_to_all(states.reshape((peer_count, slot_cap) + states.shape[1:]),...]
    unnamed x74 -> x68, local copies, waits for them, and re-layouts: 15.3 us -> 12.1 us
  transfers between devices with their start and end apart: 2 -> 1, of which waited for: 1 -> 0; matrix products, arithmetic and copies ran while one was open for 5% -> 4% of each run, Pallas kernels for 52% -> 54%
where the time goes in v3:
time: 104 us
  Pallas kernels  78.1 us (75%)
  local copies, waits for them, and re-layouts  14.4 us (14%)
  starting transfers between devices  7.66 us (7%)
  other arithmetic  2.32 us (2%)
    pallas_call x1, Pallas kernels, send_home(): pl.pallas_call(functools.partial(home_kernel, peers), out_shape=jax.Shape...  20.2 us
    pallas_call x1, Pallas kernels, trade(): pl.pallas_call(functools.partial(trade_kernel, peers, cap), in_specs=[pl....  14.8 us
    pallas_call x1, Pallas kernels, attend_resident(): pl.pallas_call(resident_kernel, grid_spec=pltpu.PrefetchScalarGridSpec(nu...  13.5 us
    unnamed x68, local copies, waits for them, and re-layouts  12.1 us
    all_to_all x1, starting transfers between devices, shards(): lax.all_to_all(states.reshape((peer_count, slot_cap) + states.shape[1:]),...  7.66 us
    pallas_call x1, Pallas kernels, update_late(): pl.pallas_call(late_kernel, grid_spec=pltpu.PrefetchScalarGridSpec(num_sc...  7.14 us
    pallas_call x1, Pallas kernels, step_sizes(): pl.pallas_call(functools.partial(step_kernel, count), out_shape=(jax.Shap...  6.27 us
    pallas_call x1, Pallas kernels, update_early(): pl.pallas_call(functools.partial(early_kernel, late), grid_spec=pltpu.Pre...  6.27 us
  transfers between devices with their start and end apart: 1, of which 0 were waited for; matrix products, arithmetic and copies ran while one was open for 4% of the time, Pallas kernels for 54%

profile of v3, /device:TPU:0, one launch (start us, length us, event | category | flops | bytes accessed | tf_op | source)
XLA Modules:
  0.0 103.6 jit_solution(12176281595210053224)
XLA Ops:
  0.6 0.8 copy.37
  1.4 0.1 broadcast_in_dim_reshape_squeeze.3.line_hbm
  1.5 0.1 reshape_squeeze.9.slots_ref
  1.5 0.9 copy-done.9
  2.5 1.0 copy-done.11
  3.5 0.8 copy-done.14
  4.2 0.7 copy-done.19
  4.9 0.7 copy-done.21
  5.5 0.0 copy-start.20
  5.5 0.0 copy-start.22
  5.6 14.8 %trade.1 = (bf16[8,2,14848]{2,1,0:T(2,128)(2,1)S(1)}, bf16[16,16,4096]{2,1,0:T(8,128)(2,1)S(1)}) custom-call(s32[16]{0:T(128)S(1)} %reshape_squeeze.9.slots_ref, s32[1,32]{1,0:T(1,128)S(1)} %bitcast.44, s32[1,32]{1,0:T(1,128)S(1)} %bitcast.46, s32[1,16]{1,0:T(1,128)S(1)} %broadcast_in_dim_reshape_squeeze.3.line_hbm, bf16[3,16,4096]{2,1,0:T(8,128)(2,1)S(1)} %bitcast.37, ...), custom_call_target="tpu_custom_call" | custom-call | flops 6291456 | bytes 6291456 | tf_op jit(solution)/shard_map/trade/pallas_call | solution.py:253
  20.4 0.0 copy-start.4
  20.4 1.3 %copy-done.4 = bf16[16,16,4096]{2,1,0:T(8,128)(2,1)} copy-done((bf16[16,16,4096]{2,1,0:T(8,128)(2,1)}, bf16[16,16,4096]{2,1,0:T(8,128)(2,1)S(1)}, u32[]{:S(2)}) %copy-start.4) | copy-done | bytes 2097176
  21.7 7.7 %all-to-all-start = ((bf16[8,2,16,4096]{3,2,1,0:T(8,128)(2,1)}), bf16[8,2,16,4096]{3,2,1,0:T(8,128)(2,1)S(1)}, u32[]{:S(2)}, u32[]{:S(2)}) async-start(bf16[8,2,16,4096]{3,2,1,0:T(8,128)(2,1)} %bitcast.32), calls=%async_computation | async-start | bytes 4194304 | tf_op jit(solution)/shard_map/all_to_all | solution.py:654
  29.4 0.0 copy-start.23
  29.4 0.2 reshape.43.got_ref
  29.7 0.0 copy-done.30
  29.7 0.1 copy.39
  29.8 0.6 reshape_squeeze.10.lens
  30.4 0.0 copy-done.29
  30.4 0.1 reshape_squeeze.11.pages
  30.4 0.0 copy-done.15
  30.5 0.0 copy-done.16
  30.5 0.0 copy-done.20
  30.5 0.0 copy-done.22
  30.5 0.0 copy-start.6
  30.5 1.3 %copy-done.6 = bf16[32,3,4096]{2,0,1:T(8,128)(2,1)S(1)} copy-done((bf16[32,3,4096]{2,0,1:T(8,128)(2,1)S(1)}, bf16[32,3,4096]{2,0,1:T(8,128)(2,1)}, u32[]{:S(2)}) %copy-start.6) | copy-done | bytes 786456
  31.8 1.1 %copy-done.13 = bf16[32,4096]{1,0:T(8,128)(2,1)S(1)} copy-done((bf16[32,4096]{1,0:T(8,128)(2,1)S(1)}, bf16[32,4096]{1,0:T(8,128)(2,1)}, u32[]{:S(2)}) %copy-start.13) | copy-done | bytes 262168
  32.9 4.2 %conv_proj.1 = (f32[32,4096]{1,0:T(8,128)S(1)}, bf16[3,32,4096]{2,1,0:T(8,128)(2,1)}, f32[32,544]{1,0:T(8,128)S(1)}) custom-call(s32[1,32]{1,0:T(1,128)S(1)} %bitcast.45, s32[1,32]{1,0:T(1,128)S(1)} %bitcast.47, bf16[32,4096]{1,0:T(8,128)(2,1)S(1)} %copy-done.13, bf16[3,32,4096]{2,1,0:T(8,128)(2,1)S(1)} %bitcast.33, bf16[16,14848]{1,0:T(8,128)(2,1)S(1)} %reshape.43.got_ref, ...), custom_call_target="tpu_custom_call" | custom-call | flops 142606336 | bytes 6553600 | tf_op jit(solution)/shard_map/conv_proj/pallas_call | solution.py:351
  37.1 0.0 copy-done.17
  37.1 0.0 copy-done.23
  37.1 0.0 copy-done
  37.1 0.0 copy-start.26
  37.1 0.6 copy-done.26
  37.8 0.7 copy-done.27
  38.4 6.3 %tp_sum_step.1 = (f32[32,4096]{1,0:T(8,128)S(1)}, f32[2,32,16]{2,1,0:T(8,128)S(1)}) custom-call(f32[32,544]{1,0:T(8,128)S(1)} %get-tuple-element.21.part_ref, bf16[512,4096]{1,0:T(8,128)(2,1)S(1)} %copy-done, f32[1,4096]{1,0:T(1,128)S(1)} %bitcast.42, f32[1,512]{1,0:T(1,128)S(1)} %bitcast.48, f32[1,16]{1,0:T(1,128)S(1)} %bitcast.49, f32[1,16]{1,0:T(1,128)S(1)} %bitcast.50), custom_call_target="tpu_custom_call" | custom-call | flops 134217728 | bytes 4718592 | tf_op jit(solution)/shard_map/tp_sum_step/pallas_call | solution.py:407
  44.7 0.0 copy-start.2
  44.7 0.2 convert_reduce_fusion
  44.9 0.6 broadcast_maximum_fusion
  45.6 0.6 add_select_fusion
  46.2 0.1 select_reduce_fusion.perm
  46.3 0.0 copy-done.5
  46.3 0.0 copy-start.1
  46.3 0.0 copy-start.24
  46.4 6.3 %ssm_early.1 = (f32[32,16,4096]{2,1,0:T(8,128)}, f32[32,4096]{1,0:T(8,128)S(1)}) custom-call(s32[32]{0:T(128)S(1)} %select_reduce_fusion.perm, f32[32,16,4096]{2,1,0:T(8,128)} %refs_3_.3, f32[32,16,4096]{2,1,0:T(8,128)} %refs_3_.3, f32[32,16,4096]{2,1,0:T(8,128)} %refs_3_.3, f32[32,16,4096]{2,1,0:T(8,128)} %refs_3_.3, ...), custom_call_target="tpu_custom_call" | custom-call | flops 8388608 | bytes 8388608 | tf_op jit(solution)/shard_map/ssm_early/pallas_call | solution.py:532
  52.6 0.0 copy-done.2
  52.6 0.0 copy-start.7
  52.7 0.0 copy-start.10
  52.7 0.0 copy-start.25
  52.7 0.0 copy-done.1
  52.7 0.0 copy-done.24
  52.7 5.7 %attend_paged.1 = bf16[16,16,128]{2,1,0:T(8,128)(2,1)S(1)} custom-call(s32[16]{0:T(128)S(1)} %copy-done.24, s32[512]{0:T(512)S(1)} %reshape_squeeze.11.pages, bf16[16,16,128]{2,1,0:T(8,128)(2,1)S(1)} %bitcast.38, bf16[256,16,512]{2,1,0:T(8,128)(2,1)S(1)} %copy-done.1, bf16[16,4,128]{2,1,0:T(4,128)(2,1)S(1)} %reshape.45.nkv_ref), custom_call_target="tpu_custom_call" | custom-call | flops 134217728 | bytes 4194304 | tf_op jit(solution)/shard_map/attend_paged/pallas_call | solution.py:132
  58.5 0.0 copy-done.7
  58.5 20.2 %send_home.1 = bf16[8,2,16,128]{3,2,1,0:T(8,128)(2,1)S(1)} custom-call(bf16[8,2,16,128]{3,2,1,0:T(8,128)(2,1)S(1)} %bitcast.39), custom_call_target="tpu_custom_call" | custom-call | bytes 131072 | tf_op jit(solution)/shard_map/send_home/pallas_call | solution.py:304
  78.7 0.0 copy-done.10
  78.7 1.3 %gather_fusion = bf16[32,2048]{1,0:T(8,128)(2,1)} fusion(bf16[16,2048]{1,0:T(8,128)(2,1)S(1)} %bitcast.51, s32[1024]{0:T(1024)S(1)} %pad_clamp_fusion), kind=kCustom, calls=%fused_computation | custom fusion | bytes 262272 | tf_op jit(solution)/shard_map/jit(_take)/gather | solution.py:690
  80.0 0.0 copy-done.25
  80.0 13.5 %attend_resident.1 = bf16[32,16,128]{2,1,0:T(8,128)(2,1)S(1)} custom-call(s32[32]{0:T(128)S(1)} %copy-done.25, bf16[32,16,128]{2,1,0:T(8,128)(2,1)S(1)} %bitcast.34, bf16[32,512,512]{2,1,0:T(8,128)(2,1)} %kv_ref.1, bf16[32,4,128]{2,1,0:T(4,128)(2,1)S(1)} %reshape.49.nkv_ref), custom_call_target="tpu_custom_call" | custom-call | flops 268435456 | bytes 16777216 | tf_op jit(solution)/shard_map/attend_resident/pallas_call | solution.py:106
  93.6 0.0 copy-done.28
  93.6 0.7 bitcast_select_fusion
  94.3 0.0 all-to-all-done
  94.3 1.0 copy-done.3
  95.4 1.0 %copy-done.8 = f32[32,4096]{1,0:T(8,128)S(1)} copy-done((f32[32,4096]{1,0:T(8,128)S(1)}, f32[32,4096]{1,0:T(8,128)}, u32[]{:S(2)}) %copy-start.8) | copy-done | bytes 524312
  96.4 7.1 %ssm_late.1 = (f32[32,16,4096]{2,1,0:T(8,128)}, bf16[32,4096]{1,0:T(8,128)(2,1)}) custom-call(s32[32]{0:T(128)S(1)} %select_reduce_fusion.perm, s32[32]{0:T(128)S(1)} %get-tuple-element.35.source, f32[32,16,4096]{2,1,0:T(8,128)} %refs_3_.3, f32[32,16,4096]{2,1,0:T(8,128)} %refs_3_.3, f32[32,16,4096]{2,1,0:T(8,128)} %refs_3_.3, ...), custom_call_target="tpu_custom_call", output_to_operand_aliasing={{0}: (17, {})} | custom-call | flops 8388608 | bytes 10485760 | tf_op jit(solution)/shard_map/ssm_late/pallas_call | solution.py:571
  (30 shorter events, 0.1 us)
Async XLA Ops:
  1.5 0.9 copy-start.9
  2.5 1.0 copy-start.11
  3.5 0.8 copy-start.14
  4.2 0.7 copy-start.19
  4.9 0.7 copy-start.21
  5.5 24.2 %copy-start.30 = (s32[1,8,2]{1,2,0:T(2,128)S(1)}, s32[1,8,2]{1,2,0:T(2,128)}, u32[]{:S(2)}) copy-start(s32[1,8,2]{1,2,0:T(2,128)} %param.50) | copy-start | bytes 196
  5.5 24.8 %copy-start.29 = (s32[1,8,2,32]{3,2,1,0:T(2,128)S(1)}, s32[1,8,2,32]{3,2,1,0:T(2,128)}, u32[]{:S(2)}) copy-start(s32[1,8,2,32]{3,2,1,0:T(2,128)} %param.51) | copy-start | bytes 6148
  5.5 24.9 %copy-start.15 = (bf16[4,4096]{1,0:T(4,128)(2,1)S(1)}, bf16[4,4096]{1,0:T(4,128)(2,1)}, u32[]{:S(2)}) copy-start(bf16[4,4096]{1,0:T(4,128)(2,1)} %weight_ref.1) | copy-start | bytes 98308
  5.5 24.9 %copy-start.16 = (f32[4096]{0:T(1024)S(1)}, f32[4096]{0:T(1024)}, u32[]{:S(2)}) copy-start(f32[4096]{0:T(1024)} %param.33) | copy-start | bytes 49156
  5.5 24.9 %copy-start.20 = (s32[32]{0:T(128)S(1)}, s32[32]{0:T(128)}, u32[]{:S(2)}) copy-start(s32[32]{0:T(128)} %param.47) | copy-start | bytes 388
  5.5 24.9 %copy-start.22 = (s32[32]{0:T(128)S(1)}, s32[32]{0:T(128)}, u32[]{:S(2)}) copy-start(s32[32]{0:T(128)} %param.48) | copy-start | bytes 388
  20.4 1.4 %copy-start.4 = (bf16[16,16,4096]{2,1,0:T(8,128)(2,1)}, bf16[16,16,4096]{2,1,0:T(8,128)(2,1)S(1)}, u32[]{:S(2)}) copy-start(bf16[16,16,4096]{2,1,0:T(8,128)(2,1)S(1)} %get-tuple-element.19) | copy-start | bytes 6291460
  21.7 72.6 %all-to-all-start = ((bf16[8,2,16,4096]{3,2,1,0:T(8,128)(2,1)}), bf16[8,2,16,4096]{3,2,1,0:T(8,128)(2,1)S(1)}, u32[]{:S(2)}, u32[]{:S(2)}) async-start(bf16[8,2,16,4096]{3,2,1,0:T(8,128)(2,1)} %bitcast.32), calls=%async_computation | async-start | bytes 4194304 | tf_op jit(solution)/shard_map/all_to_all | solution.py:654
  29.4 7.7 %copy-start.17 = (f32[4096]{0:T(1024)S(1)}, f32[4096]{0:T(1024)}, u32[]{:S(2)}) copy-start(f32[4096]{0:T(1024)} %param.39) | copy-start | bytes 49156
  29.4 7.7 %copy-start.23 = (f32[512]{0:T(512)S(1)}, f32[512]{0:T(512)}, u32[]{:S(2)}) copy-start(f32[512]{0:T(512)} %param.35) | copy-start | bytes 6148
  30.4 6.7 %copy-start = (bf16[512,4096]{1,0:T(8,128)(2,1)S(1)}, bf16[512,4096]{1,0:T(8,128)(2,1)}, u32[]{:S(2)}) copy-start(bf16[512,4096]{1,0:T(8,128)(2,1)} %dt_proj_ref.1) | copy-start | bytes 12582916
  30.5 1.3 %copy-start.6 = (bf16[32,3,4096]{2,0,1:T(8,128)(2,1)S(1)}, bf16[32,3,4096]{2,0,1:T(8,128)(2,1)}, u32[]{:S(2)}) copy-start(bf16[32,3,4096]{2,0,1:T(8,128)(2,1)} %param.28) | copy-start | bytes 2359300
  31.8 1.1 %copy-start.13 = (bf16[32,4096]{1,0:T(8,128)(2,1)S(1)}, bf16[32,4096]{1,0:T(8,128)(2,1)}, u32[]{:S(2)}) copy-start(bf16[32,4096]{1,0:T(8,128)(2,1)} %x_ref.1) | copy-start | bytes 786436
  32.9 13.4 %copy-start.5 = (f32[16,4096]{1,0:T(8,128)S(1)}, f32[16,4096]{1,0:T(8,128)}, u32[]{:S(2)}) copy-start(f32[16,4096]{1,0:T(8,128)} %refs_11_.1) | copy-start | bytes 786436
  37.1 0.7 copy-start.26
  37.8 0.7 copy-start.27
  44.7 7.9 %copy-start.2 = (f32[32,4096]{1,0:T(8,128)}, f32[32,4096]{1,0:T(8,128)S(1)}, u32[]{:S(2)}) copy-start(f32[32,4096]{1,0:T(8,128)S(1)} %get-tuple-element.22.refs_4_.refs_8_) | copy-start | bytes 1572868
  46.3 6.4 %copy-start.1 = (bf16[256,16,512]{2,1,0:T(8,128)(2,1)S(1)}, bf16[256,16,512]{2,1,0:T(8,128)(2,1)}, u32[]{:S(2)}) copy-start(bf16[256,16,512]{2,1,0:T(8,128)(2,1)} %pool_ref.1) | copy-start | bytes 12582916
  46.3 6.3 %copy-start.24 = (s32[16]{0:T(128)S(1)}, s32[16]{0:T(128)}, u32[]{:S(2)}) copy-start(s32[16]{0:T(128)} %reshape_squeeze.10.lens) | copy-start | bytes 196
  52.6 5.8 %copy-start.7 = (f32[32,4096]{1,0:T(8,128)}, f32[32,4096]{1,0:T(8,128)S(1)}, u32[]{:S(2)}) copy-start(f32[32,4096]{1,0:T(8,128)S(1)} %get-tuple-element.28.refs_12_) | copy-start | bytes 1572868
  52.7 26.0 %copy-start.10 = (bf16[32,2048]{1,0:T(8,128)(2,1)S(1)}, bf16[32,2048]{1,0:T(8,128)(2,1)}, u32[]{:S(2)}) copy-start(bf16[32,2048]{1,0:T(8,128)(2,1)} %query_hbm.1) | copy-start | bytes 393220
  52.7 27.4 %copy-start.25 = (s32[32]{0:T(128)S(1)}, s32[32]{0:T(128)}, u32[]{:S(2)}) copy-start(s32[32]{0:T(128)} %lens.1) | copy-start | bytes 388
  80.0 13.5 %copy-start.28 = (bf16[32,2048]{1,0:T(8,128)(2,1)S(1)}, bf16[32,2048]{1,0:T(8,128)(2,1)}, u32[]{:S(2)}) copy-start(bf16[32,2048]{1,0:T(8,128)(2,1)} %gather_fusion) | copy-start | bytes 393220
  80.0 14.3 %copy-start.12 = (bf16[32,4096]{1,0:T(8,128)(2,1)S(1)}, bf16[32,4096]{1,0:T(8,128)(2,1)}, u32[]{:S(2)}) copy-start(bf16[32,4096]{1,0:T(8,128)(2,1)} %refs_14_.1) | copy-start | bytes 786436
  80.0 14.3 %copy-start.18 = (f32[4096]{0:T(1024)S(1)}, f32[4096]{0:T(1024)}, u32[]{:S(2)}) copy-start(f32[4096]{0:T(1024)} %param.41) | copy-start | bytes 49156
  94.3 1.0 %copy-start.3 = (f32[32,4096]{1,0:T(8,128)S(1)}, f32[32,4096]{1,0:T(8,128)}, u32[]{:S(2)}) copy-start(f32[32,4096]{1,0:T(8,128)} %copy-done.2) | copy-start | bytes 1572868
  95.4 1.0 %copy-start.8 = (f32[32,4096]{1,0:T(8,128)S(1)}, f32[32,4096]{1,0:T(8,128)}, u32[]{:S(2)}) copy-start(f32[32,4096]{1,0:T(8,128)} %copy-done.7) | copy-start | bytes 1572868

commit v4 on v3

--- a/solution.py
+++ b/solution.py
@@ -176,7 +176,8 @@
 
 def trade_kernel(peers, cap, slots_ref, owner_hbm, pos_hbm, line_hbm, pool_hbm, query_hbm, new_hbm,
                  states_hbm, got_ref, packed_ref, owner_ref, pos_ref, line_ref, pool_ref,
-                 query_ref, new_ref, states_ref, send_ref, load_sem, own_sem, send_sem, recv_sem):
+                 query_ref, new_ref, states_ref, send_ref, pack_ref, load_sem, own_sem, send_sem,
+                 recv_sem):
     group = lax.axis_index("rep")
     others = [lax.rem(group + k, peers) for k in range(1, peers)]
     wait_greetings = greet([{"rep": other} for other in others])
@@ -236,10 +237,13 @@
     loads[-1].wait()
 
     def pack(e, carry):
-        packed_ref[e] = states_ref[slots_ref[e]].astype(jnp.bfloat16)
+        pack_ref[e] = states_ref[slots_ref[e]].astype(jnp.bfloat16)
         return carry
 
     lax.fori_loop(0, entries, pack, 0)
+    packed = pltpu.make_async_copy(pack_ref, packed_ref, load_sem.at[len(loads)])
+    packed.start()
+    packed.wait()
     own.wait()
     for copy in copies:
         copy.wait()
@@ -253,7 +257,7 @@
     return pl.pallas_call(
         functools.partial(trade_kernel, peers, cap),
         in_specs=[pl.BlockSpec(memory_space=pltpu.SMEM)] + [anywhere] * len(operands),
-        out_specs=(anywhere, pl.BlockSpec(memory_space=pltpu.VMEM)),
+        out_specs=(anywhere, anywhere),
         out_shape=(
             jax.ShapeDtypeStruct((peers, cap, width), jnp.bfloat16),
             jax.ShapeDtypeStruct((entries,) + states.shape[1:], jnp.bfloat16),
@@ -261,12 +265,13 @@
         scratch_shapes=[pltpu.VMEM(a.shape, a.dtype) for a in operands]
         + [
             pltpu.VMEM((peers, cap, width), jnp.bfloat16),
-            pltpu.SemaphoreType.DMA((len(operands),)),
+            pltpu.VMEM((entries,) + states.shape[1:], jnp.bfloat16),
+            pltpu.SemaphoreType.DMA((len(operands) + 1,)),
             pltpu.SemaphoreType.DMA,
             pltpu.SemaphoreType.DMA((peers - 1,)),
             pltpu.SemaphoreType.DMA((peers - 1,)),
         ],
-        compiler_params=params(collective_id=1, has_side_effects=True),
+        compiler_params=pltpu.CompilerParams(collective_id=1, has_side_effects=True),
         cost_estimate=pl.CostEstimate(
             flops=2 * entries * pool.size, bytes_accessed=6 * states.size, transcendentals=0
         ),
@@ -589,7 +594,7 @@
             jax.ShapeDtypeStruct(dt.shape, jnp.bfloat16),
         ),
         input_output_aliases={2 + 2 * BATCH + len(shared): 0},
-        compiler_params=params(),
+        compiler_params=pltpu.CompilerParams(),
         cost_estimate=pl.CostEstimate(
             flops=8 * late * state[0].size,
             bytes_accessed=10 * late * state[0].size,
@@ -683,7 +688,7 @@
         kept, early_y = update_early(perm, ssm_state, dt_step, mixed, bc, decay_rate, late)
     else:
         kept, early_y = jnp.zeros_like(ssm_state), jnp.zeros_like(dt_step)
-    attn_there, early_y = lax.optimization_barrier((attn_there, early_y))
+    attn_there, attn_here, early_y = lax.optimization_barrier((attn_there, attn_here, early_y))
     attn_back = send_home(attn_there.reshape(peer_count, slot_cap, head_count, HD))
     attn_back, early_y = lax.optimization_barrier((attn_back, early_y))
     attn_back = attn_back.reshape(entry_count, query_width)

time: 104 us -> 85.2 us (0.82)
  local copies, waits for them, and re-layouts: 14.4 us -> 4.05 us
  Pallas kernels: 78.1 us -> 69.7 us
    pallas_call x1, Pallas kernels: 20.2 us -> 9.14 us  [send_home(): pl.pallas_call(functools.partial(home_kernel, peers), out_shape=jax.Shape...]
    unnamed x68 -> x55, local copies, waits for them, and re-layouts: 12.1 us -> 1.84 us
    pallas_call x1, Pallas kernels: 7.14 us -> 8.66 us  [update_late(): pl.pallas_call(late_kernel, grid_spec=pltpu.PrefetchScalarGridSpec(num_sc...]
  transfers between devices with their start and end apart: 1 -> 1, of which waited for: 0 -> 0; matrix products, arithmetic and copies ran while one was open for 4% -> 5% of each run, Pallas kernels for 54% -> 53%
where the time goes in v4:
time: 85.2 us; the launch traced here: 84.9 us
  Pallas kernels  69.7 us (82%)
  starting transfers between devices  7.34 us (9%)
  local copies, waits for them, and re-layouts  4.05 us (5%)
  other arithmetic  2.8 us (3%)
  between operations  1.1 us (1%)
    pallas_call x1, Pallas kernels, trade(): pl.pallas_call(functools.partial(trade_kernel, peers, cap), in_specs=[pl....  15.6 us
    pallas_call x1, Pallas kernels, attend_resident(): pl.pallas_call(resident_kernel, grid_spec=pltpu.PrefetchScalarGridSpec(nu...  13.5 us
    pallas_call x1, Pallas kernels, send_home(): pl.pallas_call(functools.partial(home_kernel, peers), out_shape=jax.Shape...  9.14 us
    pallas_call x1, Pallas kernels, update_late(): pl.pallas_call(late_kernel, grid_spec=pltpu.PrefetchScalarGridSpec(num_sc...  8.66 us
    all_to_all x1, starting transfers between devices, shards(): lax.all_to_all(states.reshape((peer_count, slot_cap) + states.shape[1:]),...  7.34 us
    pallas_call x1, Pallas kernels, step_sizes(): pl.pallas_call(functools.partial(step_kernel, count), out_shape=(jax.Shap...  6.33 us
    pallas_call x1, Pallas kernels, update_early(): pl.pallas_call(functools.partial(early_kernel, late), grid_spec=pltpu.Pre...  6.29 us
    pallas_call x1, Pallas kernels, attend_paged(): pl.pallas_call(paged_kernel, grid_spec=pltpu.PrefetchScalarGridSpec(num_s...  5.75 us
  transfers between devices with their start and end apart: 1, of which 0 were waited for; matrix products, arithmetic and copies ran while one was open for 5% of the time, Pallas kernels for 53%

profile of v4, /device:TPU:0, one launch (start us, length us, event | category | flops | bytes accessed | tf_op | source)
XLA Modules:
  0.0 84.9 jit_solution(307760403280504266)
XLA Ops:
  0.6 0.8 copy.37
  1.4 0.6 broadcast_in_dim_reshape_squeeze.3.line_hbm
  2.0 0.6 reshape_squeeze.9.slots_ref
  2.6 0.0 copy-start.16
  2.6 15.6 %trade.1 = (bf16[8,2,14848]{2,1,0:T(2,128)(2,1)}, bf16[16,16,4096]{2,1,0:T(8,128)(2,1)}) custom-call(s32[16]{0:T(128)} %reshape_squeeze.9.slots_ref, s32[1,32]{1,0:T(1,128)} %bitcast.37, s32[1,32]{1,0:T(1,128)} %bitcast.39, s32[1,16]{1,0:T(1,128)} %broadcast_in_dim_reshape_squeeze.3.line_hbm, bf16[3,16,4096]{2,1,0:T(8,128)(2,1)} %bitcast.49, ...), custom_call_target="tpu_custom_call" | custom-call | flops 6291456 | bytes 6291456 | tf_op jit(solution)/shard_map/trade/pallas_call | solution.py:257
  18.2 0.0 copy-start.20
  18.3 7.3 %all-to-all-start = ((bf16[8,2,16,4096]{3,2,1,0:T(8,128)(2,1)}), bf16[8,2,16,4096]{3,2,1,0:T(8,128)(2,1)}, u32[]{:S(2)}, u32[]{:S(2)}) async-start(bf16[8,2,16,4096]{3,2,1,0:T(8,128)(2,1)} %bitcast.46), calls=%async_computation | async-start | bytes 4194304 | tf_op jit(solution)/shard_map/all_to_all | solution.py:659
  25.6 0.0 copy-done.21
  25.6 0.0 copy-done.20
  25.6 0.2 reshape.43.got_ref
  25.9 0.0 copy-done.23
  25.9 0.1 copy.39
  26.0 0.1 reshape_squeeze.10.lens
  26.1 0.0 copy-done.22
  26.1 0.1 reshape_squeeze.11.pages
  26.1 0.0 copy-done.19
  26.2 0.0 copy-done.16
  26.2 0.0 copy-start.5
  26.2 0.0 copy-start.7
  26.2 0.0 copy-start.9
  26.2 0.0 copy-start.10
  26.2 0.0 copy-start.12
  26.2 0.0 copy-start.13
  26.3 13.5 %attend_resident.1 = bf16[32,16,128]{2,1,0:T(8,128)(2,1)S(1)} custom-call(s32[32]{0:T(128)S(1)} %copy-done.16, bf16[32,16,128]{2,1,0:T(8,128)(2,1)S(1)} %bitcast.31, bf16[32,512,512]{2,1,0:T(8,128)(2,1)} %kv_ref.1, bf16[32,4,128]{2,1,0:T(4,128)(2,1)S(1)} %reshape.47.nkv_ref), custom_call_target="tpu_custom_call" | custom-call | flops 268435456 | bytes 16777216 | tf_op jit(solution)/shard_map/attend_resident/pallas_call | solution.py:106
  39.8 0.0 copy-start
  39.8 0.0 copy-start.11
  39.8 0.0 copy-start.14
  39.8 0.0 copy-start.17
  39.8 0.0 copy-start.18
  39.9 0.0 copy-done.5
  39.9 0.0 copy-done.7
  39.9 0.0 copy-done.9
  39.9 0.0 copy-done.10
  39.9 0.0 copy-done.12
  39.9 0.0 copy-done.13
  39.9 0.0 copy-start.4
  40.0 4.3 %conv_proj.1 = (f32[32,4096]{1,0:T(8,128)S(1)}, bf16[3,32,4096]{2,1,0:T(8,128)(2,1)}, f32[32,544]{1,0:T(8,128)S(1)}) custom-call(s32[1,32]{1,0:T(1,128)S(1)} %bitcast.38, s32[1,32]{1,0:T(1,128)S(1)} %bitcast.40, bf16[32,4096]{1,0:T(8,128)(2,1)S(1)} %copy-done.7, bf16[3,32,4096]{2,1,0:T(8,128)(2,1)S(1)} %bitcast.29, bf16[16,14848]{1,0:T(8,128)(2,1)S(1)} %reshape.43.got_ref, ...), custom_call_target="tpu_custom_call" | custom-call | flops 142606336 | bytes 6553600 | tf_op jit(solution)/shard_map/conv_proj/pallas_call | solution.py:356
  44.3 0.0 copy-start.2
  44.3 0.0 copy-done
  44.3 0.0 copy-done.11
  44.3 0.0 copy-done.14
  44.3 0.0 copy-done.17
  44.3 0.0 copy-done.18
  44.3 6.3 %tp_sum_step.1 = (f32[32,4096]{1,0:T(8,128)S(1)}, f32[2,32,16]{2,1,0:T(8,128)S(1)}) custom-call(f32[32,544]{1,0:T(8,128)S(1)} %get-tuple-element.22.part_ref, bf16[512,4096]{1,0:T(8,128)(2,1)S(1)} %copy-done, f32[1,4096]{1,0:T(1,128)S(1)} %bitcast.36, f32[1,512]{1,0:T(1,128)S(1)} %bitcast.41, f32[1,16]{1,0:T(1,128)S(1)} %bitcast.42, f32[1,16]{1,0:T(1,128)S(1)} %bitcast.43), custom_call_target="tpu_custom_call" | custom-call | flops 134217728 | bytes 4718592 | tf_op jit(solution)/shard_map/tp_sum_step/pallas_call | solution.py:412
  50.7 0.0 copy-start.3
  50.7 0.0 copy-start.8
  50.7 0.2 convert_reduce_fusion
  50.9 1.1 %broadcast_maximum_fusion = (s32[32]{0:T(128)S(1)}, s32[32]{0:T(128)}, s32[]{:T(128)}) fusion(s32[32]{0:T(128)S(1)} %copy-done.13, s32[32]{0:T(128)S(1)} %copy-done.12), kind=kLoop, calls=%fused_computation.14 | loop fusion | flops 223 | bytes 516 | tf_op jit(solution)/shard_map/max | solution.py:695
  52.0 0.6 add_select_fusion
  52.7 0.1 select_reduce_fusion.perm
  52.8 0.0 copy-done.4
  52.8 0.0 copy-start.1
  52.8 6.3 %ssm_early.1 = (f32[32,16,4096]{2,1,0:T(8,128)}, f32[32,4096]{1,0:T(8,128)S(1)}) custom-call(s32[32]{0:T(128)S(1)} %select_reduce_fusion.perm, f32[32,16,4096]{2,1,0:T(8,128)} %refs_3_.3, f32[32,16,4096]{2,1,0:T(8,128)} %refs_3_.3, f32[32,16,4096]{2,1,0:T(8,128)} %refs_3_.3, f32[32,16,4096]{2,1,0:T(8,128)} %refs_3_.3, ...), custom_call_target="tpu_custom_call" | custom-call | flops 8388608 | bytes 8388608 | tf_op jit(solution)/shard_map/ssm_early/pallas_call | solution.py:537
  59.1 0.0 copy-done.2
  59.1 0.0 copy-done.3
  59.1 0.0 copy-done.8
  59.1 0.0 copy-done.15
  59.2 0.8 copy-done.6
  59.9 5.7 %attend_paged.1 = bf16[16,16,128]{2,1,0:T(8,128)(2,1)S(1)} custom-call(s32[16]{0:T(128)S(1)} %reshape_squeeze.10.lens, s32[512]{0:T(512)S(1)} %reshape_squeeze.11.pages, bf16[16,16,128]{2,1,0:T(8,128)(2,1)S(1)} %bitcast.32, bf16[256,16,512]{2,1,0:T(8,128)(2,1)S(1)} %copy-done.1, bf16[16,4,128]{2,1,0:T(4,128)(2,1)S(1)} %reshape.45.nkv_ref), custom_call_target="tpu_custom_call" | custom-call | flops 134217728 | bytes 4194304 | tf_op jit(solution)/shard_map/attend_paged/pallas_call | solution.py:132
  65.7 9.1 %send_home.1 = bf16[8,2,16,128]{3,2,1,0:T(8,128)(2,1)S(1)} custom-call(bf16[8,2,16,128]{3,2,1,0:T(8,128)(2,1)S(1)} %bitcast.33), custom_call_target="tpu_custom_call" | custom-call | bytes 131072 | tf_op jit(solution)/shard_map/send_home/pallas_call | solution.py:309
  74.9 0.7 gather_fusion
  75.5 0.7 broadcast_select_fusion
  76.3 0.0 all-to-all-done
  76.3 8.7 %ssm_late.1 = (f32[32,16,4096]{2,1,0:T(8,128)}, bf16[32,4096]{1,0:T(8,128)(2,1)}) custom-call(s32[32]{0:T(128)} %copy-done.15, s32[32]{0:T(128)} %get-tuple-element.37.source, f32[32,16,4096]{2,1,0:T(8,128)} %refs_3_.3, f32[32,16,4096]{2,1,0:T(8,128)} %refs_3_.3, f32[32,16,4096]{2,1,0:T(8,128)} %refs_3_.3, ...), custom_call_target="tpu_custom_call", output_to_operand_aliasing={{0}: (17, {})} | custom-call | flops 8388608 | bytes 10485760 | tf_op jit(solution)/shard_map/ssm_late/pallas_call | solution.py:576
  (17 shorter events, 0.1 us)
Async XLA Ops:
  2.6 23.0 %copy-start.21 = (bf16[32,512]{1,0:T(8,128)(2,1)S(1)}, bf16[32,512]{1,0:T(8,128)(2,1)}, u32[]{:S(2)}) copy-start(bf16[32,512]{1,0:T(8,128)(2,1)} %new_hbm.1) | copy-start | bytes 98308
  2.6 23.3 %copy-start.23 = (s32[1,8,2]{1,2,0:T(2,128)S(1)}, s32[1,8,2]{1,2,0:T(2,128)}, u32[]{:S(2)}) copy-start(s32[1,8,2]{1,2,0:T(2,128)} %param.50) | copy-start | bytes 196
  2.6 23.5 %copy-start.22 = (s32[1,8,2,32]{3,2,1,0:T(2,128)S(1)}, s32[1,8,2,32]{3,2,1,0:T(2,128)}, u32[]{:S(2)}) copy-start(s32[1,8,2,32]{3,2,1,0:T(2,128)} %param.51) | copy-start | bytes 6148
  2.6 23.6 %copy-start.19 = (bf16[32,2048]{1,0:T(8,128)(2,1)S(1)}, bf16[32,2048]{1,0:T(8,128)(2,1)}, u32[]{:S(2)}) copy-start(bf16[32,2048]{1,0:T(8,128)(2,1)} %query_hbm.1) | copy-start | bytes 393220
  2.6 23.6 %copy-start.16 = (s32[32]{0:T(128)S(1)}, s32[32]{0:T(128)}, u32[]{:S(2)}) copy-start(s32[32]{0:T(128)} %lens.1) | copy-start | bytes 388
  18.2 7.4 %copy-start.20 = (bf16[8,2,14848]{2,1,0:T(2,128)(2,1)S(1)}, bf16[8,2,14848]{2,1,0:T(2,128)(2,1)}, u32[]{:S(2)}) copy-start(bf16[8,2,14848]{2,1,0:T(2,128)(2,1)} %get-tuple-element.21) | copy-start | bytes 1425412
  18.3 58.0 %all-to-all-start = ((bf16[8,2,16,4096]{3,2,1,0:T(8,128)(2,1)}), bf16[8,2,16,4096]{3,2,1,0:T(8,128)(2,1)}, u32[]{:S(2)}, u32[]{:S(2)}) async-start(bf16[8,2,16,4096]{3,2,1,0:T(8,128)(2,1)} %bitcast.46), calls=%async_computation | async-start | bytes 4194304 | tf_op jit(solution)/shard_map/all_to_all | solution.py:659
  26.2 13.7 %copy-start.5 = (bf16[32,3,4096]{2,0,1:T(8,128)(2,1)S(1)}, bf16[32,3,4096]{2,0,1:T(8,128)(2,1)}, u32[]{:S(2)}) copy-start(bf16[32,3,4096]{2,0,1:T(8,128)(2,1)} %param.28) | copy-start | bytes 2359300
  26.2 13.7 %copy-start.7 = (bf16[32,4096]{1,0:T(8,128)(2,1)S(1)}, bf16[32,4096]{1,0:T(8,128)(2,1)}, u32[]{:S(2)}) copy-start(bf16[32,4096]{1,0:T(8,128)(2,1)} %x_ref.1) | copy-start | bytes 786436
  26.2 13.7 %copy-start.9 = (bf16[4,4096]{1,0:T(4,128)(2,1)S(1)}, bf16[4,4096]{1,0:T(4,128)(2,1)}, u32[]{:S(2)}) copy-start(bf16[4,4096]{1,0:T(4,128)(2,1)} %weight_ref.1) | copy-start | bytes 98308
  26.2 13.7 %copy-start.10 = (f32[4096]{0:T(1024)S(1)}, f32[4096]{0:T(1024)}, u32[]{:S(2)}) copy-start(f32[4096]{0:T(1024)} %param.33) | copy-start | bytes 49156
  26.2 13.7 %copy-start.12 = (s32[32]{0:T(128)S(1)}, s32[32]{0:T(128)}, u32[]{:S(2)}) copy-start(s32[32]{0:T(128)} %param.47) | copy-start | bytes 388
  26.2 13.7 %copy-start.13 = (s32[32]{0:T(128)S(1)}, s32[32]{0:T(128)}, u32[]{:S(2)}) copy-start(s32[32]{0:T(128)} %param.48) | copy-start | bytes 388
  39.8 4.5 %copy-start = (bf16[512,4096]{1,0:T(8,128)(2,1)S(1)}, bf16[512,4096]{1,0:T(8,128)(2,1)}, u32[]{:S(2)}) copy-start(bf16[512,4096]{1,0:T(8,128)(2,1)} %dt_proj_ref.1) | copy-start | bytes 12582916
  39.8 4.5 %copy-start.11 = (f32[4096]{0:T(1024)S(1)}, f32[4096]{0:T(1024)}, u32[]{:S(2)}) copy-start(f32[4096]{0:T(1024)} %param.39) | copy-start | bytes 49156
  39.8 4.5 %copy-start.14 = (f32[512]{0:T(512)S(1)}, f32[512]{0:T(512)}, u32[]{:S(2)}) copy-start(f32[512]{0:T(512)} %param.35) | copy-start | bytes 6148
  39.8 4.5 %copy-start.17 = (f32[16]{0:T(128)S(1)}, f32[16]{0:T(128)}, u32[]{:S(2)}) copy-start(f32[16]{0:T(128)} %param.36) | copy-start | bytes 196
  39.8 4.5 %copy-start.18 = (f32[16]{0:T(128)S(1)}, f32[16]{0:T(128)}, u32[]{:S(2)}) copy-start(f32[16]{0:T(128)} %param.37) | copy-start | bytes 196
  39.9 12.8 %copy-start.4 = (f32[16,4096]{1,0:T(8,128)S(1)}, f32[16,4096]{1,0:T(8,128)}, u32[]{:S(2)}) copy-start(f32[16,4096]{1,0:T(8,128)} %refs_11_.1) | copy-start | bytes 786436
  44.3 14.8 %copy-start.2 = (f32[32,4096]{1,0:T(8,128)}, f32[32,4096]{1,0:T(8,128)S(1)}, u32[]{:S(2)}) copy-start(f32[32,4096]{1,0:T(8,128)S(1)} %get-tuple-element.24.refs_5_.refs_9_) | copy-start | bytes 1572868
  50.7 8.4 %copy-start.3 = (f32[32,4096]{1,0:T(8,128)}, f32[32,4096]{1,0:T(8,128)S(1)}, u32[]{:S(2)}) copy-start(f32[32,4096]{1,0:T(8,128)S(1)} %get-tuple-element.23.refs_4_.refs_8_) | copy-start | bytes 1572868
  50.7 8.4 %copy-start.8 = (f32[2,32,16]{2,1,0:T(8,128)}, f32[2,32,16]{2,1,0:T(8,128)S(1)}, u32[]{:S(2)}) copy-start(f32[2,32,16]{2,1,0:T(8,128)S(1)} %get-tuple-element.25.refs_6_.refs_10_) | copy-start | bytes 12292
  52.8 6.4 %copy-start.15 = (s32[32]{0:T(128)}, s32[32]{0:T(128)S(1)}, u32[]{:S(2)}) copy-start(s32[32]{0:T(128)S(1)} %select_reduce_fusion.perm) | copy-start | bytes 388
  52.8 7.2 %copy-start.1 = (bf16[256,16,512]{2,1,0:T(8,128)(2,1)S(1)}, bf16[256,16,512]{2,1,0:T(8,128)(2,1)}, u32[]{:S(2)}) copy-start(bf16[256,16,512]{2,1,0:T(8,128)(2,1)} %pool_ref.1) | copy-start | bytes 12582916
  59.1 0.8 copy-start.6
